TPU v7x, 32 devices: a whole 2x2x4 slice. The times are simulated.
32 devices in a mesh: narrow: 8 (over z, y), wide: 4 (over x, core).
Axes of the slice: x: 2, y: 2, z: 4, core: 2. Of those that a mesh axis runs over, the one named last changes fastest.
Arguments:
- frame_tokens: bfloat16 [96, 197, 768], P('narrow', None, 'wide'), may hold values from -6 to 6
- cotangent: bfloat16 [96, 197, 768], P('narrow', None, 'wide'), may hold values from -6 to 6
- caption_count: int32 [12], replicated, may hold values from 1 to 5, as said below
- caption_len: int32 [12, 5], replicated, may hold values from 1 to 77, as said below
- message_weight: bfloat16 [768, 768], replicated, may hold values from -0.21875 to 0.21875
- message_bias: float32 [768], replicated, may hold values from -3 to 3
- message_gain: float32 [768], replicated, may hold values from 0.5 to 1.5
- message_shift: float32 [768], replicated, may hold values from -2 to 2
- cross_qkv: bfloat16 [768, 3, 768], P(None, None, 'wide'), may hold values from -0.21875 to 0.21875
- cross_bias: float32 [2, 768], P(None, 'wide'), may hold values from -3 to 3
- cross_proj: bfloat16 [768, 768], P('wide'), may hold values from -0.4375 to 0.4375
- cross_offset: float32 [768], replicated, may hold values from -2 to 2
- attn_gain: float32 [768], replicated, may hold values from 0.5 to 1.5
- attn_shift: float32 [768], replicated, may hold values from -2 to 2
- qkv_weight: bfloat16 [768, 3, 768], P(None, None, 'wide'), may hold values from -0.21875 to 0.21875
- qkv_bias: float32 [2, 768], P(None, 'wide'), may hold values from -3 to 3
- out_weight: bfloat16 [768, 768], P('wide'), may hold values from -1.25 to 1.25
- out_bias: float32 [768], P('wide'), may hold values from -2 to 2
- mlp_gain: float32 [768], replicated, may hold values from 0.5 to 1.5
- mlp_shift: float32 [768], replicated, may hold values from -2 to 2
- up_weight: bfloat16 [768, 3072], P(None, 'wide'), may hold values from -0.21650635 to 0.21650635
- up_bias: float32 [3072], P('wide'), may hold values from -3 to 3
- down_weight: bfloat16 [3072, 768], P('wide'), may hold values from -0.109375 to 0.109375
- down_bias: float32 [768], P('wide'), may hold values from -2 to 2
Outputs:
- output_tokens: bfloat16 [96, 197, 768], P('narrow', None, 'wide')
- grad_tokens: bfloat16 [96, 197, 768], P('narrow', None, 'wide')
- grad_message_weight: float32 [768, 768], replicated
- grad_message_bias: float32 [768], replicated
- grad_message_gain: float32 [768], replicated
- grad_message_shift: float32 [768], replicated
- grad_cross_qkv: float32 [768, 3, 768], P(None, None, 'wide')
- grad_cross_bias: float32 [2, 768], P(None, 'wide')
- grad_cross_proj: float32 [768, 768], P('wide')
- grad_cross_offset: float32 [768], replicated
- grad_attn_gain: float32 [768], replicated
- grad_attn_shift: float32 [768], replicated
- grad_qkv_weight: float32 [768, 3, 768], P(None, None, 'wide')
- grad_qkv_bias: float32 [2, 768], P(None, 'wide')
- grad_out_weight: float32 [768, 768], P('wide')
- grad_out_bias: float32 [768], P('wide')
- grad_mlp_gain: float32 [768], replicated
- grad_mlp_shift: float32 [768], replicated
- grad_up_weight: float32 [768, 3072], P(None, 'wide')
- grad_up_bias: float32 [3072], P('wide')
- grad_down_weight: float32 [3072, 768], P('wide')
- grad_down_bias: float32 [768], P('wide')
Inputs may be any that keep to these rules, and one draw needn't show every extreme that they name: Captions of each video; a video uses its first caption_count slots. `caption_len`: words of a caption slot; slots at or after a video's caption_count are unused and hold a value too.
All inputs are finite; a program needn't handle non-finite values.
Results may differ from a plain program's by a relative error of at most 0.02.
Values may be sent and summed in bfloat16 or wider, within the bound.
No kernel may reach another device: no remote copies, remote signals or barrier semaphores. Data moves between devices by JAX's collectives and lax.ppermute only.
A program may use at most 192 MiB of HBM per device.

v0:
```python
import functools
import jax
import jax.numpy as jnp
from jax import lax
from jax.experimental import pallas as pl
from jax.experimental.pallas import tpu as pltpu
from jax.sharding import PartitionSpec as P

VIDEO_FRAMES = 8
HD = 64
EPS = 1e-05
ROW_TILE = 16
LOW = jnp.bfloat16
F32 = jnp.float32
VMEM_LIMIT = 56 * 1024 * 1024
ANY = pl.BlockSpec(memory_space=pl.ANY)
VMEM = pl.BlockSpec(memory_space=pltpu.VMEM)
SMEM = pl.BlockSpec(memory_space=pltpu.SMEM)


def dot(left, right, dims):
    return lax.dot_general(left, right, (dims, ((), ())), preferred_element_type=F32)


def mat_mul(left, right):
    return dot(left, right, ((1,), (0,)))


def mat_tn(left, right):
    return dot(left, right, ((0,), (0,)))


def mat_nt(left, right):
    return dot(left, right, ((1,), (1,)))


def normalize(values):
    row_mean = jnp.mean(values, axis=-1, keepdims=True)
    centred = values - row_mean
    inv_std = lax.rsqrt(jnp.mean(centred * centred, axis=-1, keepdims=True) + EPS)
    return (centred * inv_std, inv_std)


def norm_back(grad_norm, normed, inv_std, norm_gain):
    scaled = grad_norm * norm_gain
    return inv_std * (
        scaled
        - jnp.mean(scaled, axis=-1, keepdims=True)
        - normed * jnp.mean(scaled * normed, axis=-1, keepdims=True)
    )


def bits_of(size):
    return [1 << b for b in range(size.bit_length() - 1)]


def reorder(parts, index):
    parts = list(parts)
    for bit in bits_of(len(parts)):
        odd = (index & bit) != 0
        parts = [jnp.where(odd, parts[k ^ bit], parts[k]) for k in range(len(parts))]
    return parts


def call(kernel, name, micros=0.0, **options):
    return pl.pallas_call(
        kernel,
        name=name,
        compiler_params=pltpu.CompilerParams(vmem_limit_bytes=VMEM_LIMIT),
        cost_estimate=pl.CostEstimate(
            flops=int(micros * 1.0e9), bytes_accessed=int(micros * 3.0e6), transcendentals=0
        ),
        **options,
    )


def shaped(shape, dtype):
    return jax.ShapeDtypeStruct(tuple(shape), dtype)


def whole(array):
    return pl.BlockSpec(array.shape, lambda *_: (0,) * array.ndim)


def fixed(shape):
    return pl.BlockSpec(tuple(shape), lambda *_: (0,) * len(shape))


def per_step(shape):
    return pl.BlockSpec((1,) + tuple(shape[1:]), lambda f: (f,) + (0,) * (len(shape) - 1))


def row_of(ref):
    return ref[...].reshape(1, -1)


def head_masks(width):
    lane = lax.broadcasted_iota(jnp.int32, (1, width), 1) // HD
    return [lane == h for h in range(width // HD)]


def stack_heads(values, masks, scale=1.0):
    return jnp.concatenate([values * jnp.where(m, scale, 0.0).astype(values.dtype) for m in masks], axis=0)


def pick_heads(values, masks):
    size = values.shape[0] // len(masks)
    picked = values[:size]
    for h in range(1, len(masks)):
        picked = jnp.where(masks[h], values[h * size : (h + 1) * size], picked)
    return picked


def weight_copies(refs, shards, place_ref, buf, sem):
    whole_count = 2 * shards - len(refs)
    odd = place_ref[1]
    copies = []
    for j in range(whole_count):
        copies.append([pltpu.make_async_copy(refs[j], buf.at[j], sem.at[j, 0])])
    rest = refs[whole_count:]
    for i in range(len(rest) // 2):
        half = rest[2 * i].shape[0]
        at = pl.multiple_of(odd * half, half)
        other = pl.multiple_of((1 - odd) * half, half)
        j = whole_count + i
        copies.append([
            pltpu.make_async_copy(rest[2 * i], buf.at[j, pl.ds(at, half)], sem.at[j, 0]),
            pltpu.make_async_copy(rest[2 * i + 1], buf.at[j, pl.ds(other, half)], sem.at[j, 1]),
        ])
    return copies


def start_all(copies):
    for group in copies:
        for copy in group:
            copy.start()


def wait_all(copies):
    for group in copies:
        for copy in group:
            copy.wait()


def attn_forward_kernel(waits, place_ref, gain_ref, shift_ref, mlp_gain_ref, mlp_shift_ref, base_ref, *refs):
    shards = refs[-3].shape[0]
    toks, refs = refs[:shards], refs[shards:]
    sums, refs = refs[:shards], refs[shards:]
    packs, refs = refs[:shards], refs[shards:]
    weights, refs = refs[: -14 - waits], refs[-14:]
    (normed_ref, inv_ref, attn_in_ref, heads_ref, prob_ref, mix_ref, hidden_ref, mlp_normed_ref,
     mlp_inv_ref, mlp_in_ref, tok_buf, w_buf, w_sem, msg_buf) = refs
    part, patches = toks[0].shape[1], toks[0].shape[2]
    seq_pad, width = normed_ref.shape[1], normed_ref.shape[2]
    frames = pl.num_programs(0)
    frame = pl.program_id(0)
    wide_idx = place_ref[0]
    copies = weight_copies(weights, shards, place_ref, w_buf, w_sem)

    @pl.when(frame == 0)
    def _():
        start_all(copies)
        tok_buf[...] = jnp.zeros_like(tok_buf)
        total = base_ref[...]
        for ref in sums:
            total += ref[...]
        msg_buf[...] = total

    for k in range(shards):
        at = pl.multiple_of((wide_idx ^ k) * part, part)
        tok_buf[pl.ds(at, part), :patches] = toks[k][0]
    tokens = tok_buf[...].T[:seq_pad].astype(F32)
    group = msg_buf[...]
    own = lax.broadcasted_iota(jnp.int32, (group.shape[0], 1), 0) == wide_idx * frames + frame
    message = jnp.sum(jnp.where(own, group, 0.0), axis=0, keepdims=True)
    row = lax.broadcasted_iota(jnp.int32, (seq_pad, 1), 0)
    full = jnp.where(row == patches, message, tokens)
    normed, inv = normalize(full)
    normed_ref[0] = normed
    inv_ref[0] = inv
    gain, shift, mlp_gain, mlp_shift = map(row_of, (gain_ref, shift_ref, mlp_gain_ref, mlp_shift_ref))
    attn_in = (normed * gain + shift).astype(LOW)
    attn_in_ref[0] = attn_in
    masks = head_masks(part)
    live = lax.broadcasted_iota(jnp.int32, (1, seq_pad), 1) <= patches
    total = full + jnp.concatenate(reorder([p[1:2, 2 * part : 3 * part] for p in packs], wide_idx), axis=1)

    @pl.when(frame == 0)
    def _():
        wait_all(copies)

    for k in range(shards):
        proj = mat_nt(attn_in, w_buf[k, : 3 * part])
        queries = (proj[:, :part] + packs[k][1:2, :part]).astype(LOW)
        keys = proj[:, part : 2 * part].astype(LOW)
        values = (proj[:, 2 * part :] + packs[k][1:2, part : 2 * part]).astype(LOW)
        heads_ref[0, k, 0] = queries
        heads_ref[0, k, 1] = keys
        heads_ref[0, k, 2] = values
        scores = mat_nt(stack_heads(queries, masks, HD ** (-0.5)), keys)
        scores = jnp.where(live, scores, -1e30)
        exps = jnp.exp(scores - jnp.max(scores, axis=-1, keepdims=True))
        prob = (exps * (1.0 / jnp.sum(exps, axis=-1, keepdims=True))).astype(LOW)
        prob_ref[0, k] = prob
        mix_low = pick_heads(mat_mul(prob, values), masks).astype(LOW)
        mix_ref[0, k] = mix_low
        total += mat_mul(mix_low, w_buf[k, 3 * part :])
    hidden_ref[0] = total
    mlp_normed, mlp_inv = normalize(total.astype(LOW).astype(F32))
    mlp_normed_ref[0] = mlp_normed
    mlp_inv_ref[0] = mlp_inv
    mlp_in_ref[0] = (mlp_normed * mlp_gain + mlp_shift).astype(LOW)


def attn_forward(seq_pad, place, vecs, base, toks, sums, packs, weights, after):
    frames, part, patches = toks[0].shape
    shards = len(toks)
    width = part * shards
    heads = part // HD
    seq_lanes = -(-seq_pad // 128) * 128
    shapes = [
        ((frames, seq_pad, width), F32),
        ((frames, seq_pad, 1), F32),
        ((frames, seq_pad, width), LOW),
        ((frames, shards, 3, seq_pad, part), LOW),
        ((frames, shards, heads * seq_pad, seq_pad), LOW),
        ((frames, shards, seq_pad, part), LOW),
        ((frames, seq_pad, width), F32),
        ((frames, seq_pad, width), F32),
        ((frames, seq_pad, 1), F32),
        ((frames, seq_pad, width), LOW),
    ]
    return call(
        functools.partial(attn_forward_kernel, len(after)),
        "attn_forward",
        grid=(frames,),
        in_specs=[SMEM] + [whole(v) for v in vecs] + [whole(base)]
        + [per_step(v.shape) for v in toks]
        + [whole(v) for v in list(sums) + list(packs)]
        + [ANY] * (len(weights) + len(after)),
        out_specs=[per_step(s) for s, _ in shapes],
        out_shape=[shaped(s, d) for s, d in shapes],
        scratch_shapes=[
            pltpu.VMEM((width, seq_lanes), LOW),
            pltpu.VMEM((shards, 4 * part, width), LOW),
            pltpu.SemaphoreType.DMA((shards, 2)),
            pltpu.VMEM(base.shape, F32),
        ],
    )(place, *vecs, base, *toks, *sums, *packs, *weights, *after)


def mlp_kernel(frames, count, first, waits, place_ref, scale_ref, mlp_in_ref, *refs):
    packs, refs = refs[:count], refs[count:]
    if first:
        shards = 2 * count
        cots, refs = refs[:shards], refs[shards:]
    else:
        (grad_ref, acc_in, gacc_in), refs = refs[:3], refs[3:]
    weights, refs = refs[: 2 * count], refs[2 * count + waits :]
    if first:
        (cot_ref, grad_ref), refs = refs[:2], refs[2:]
    acc_ref, gacc_ref, sums_ref = refs[:3]
    g_refs, refs = refs[3 : 3 + count], refs[3 + count :]
    w_buf, g_buf, act_buf, pre_buf, in_sem, out_sem = refs[:6]
    rows, width = mlp_in_ref.shape
    hidden = act_buf.shape[1]
    step = rows // frames
    loads = []
    for i in range(count):
        if first:
            for j, ref in ((2 * i, weights[i]), (2 * i + 1, weights[count + i])):
                loads.append([pltpu.make_async_copy(ref, w_buf.at[j], in_sem.at[j, 0])])
        else:
            half = weights[2 * i].shape[0] // 2
            for j in range(2):
                load = []
                for n, odd in enumerate((place_ref[1], 1 - place_ref[1])):
                    to = w_buf.at[2 * i + j, pl.ds(pl.multiple_of(odd * half, half), half)]
                    load.append(
                        pltpu.make_async_copy(weights[2 * i + n].at[pl.ds(j * half, half)], to, in_sem.at[2 * i + j, n])
                    )
                loads.append(load)
    start_all(loads)
    stores = [
        pltpu.make_async_copy(g_buf.at[2 * i + j], g_refs[i].at[pl.ds(j * width, width)], out_sem.at[2 * i + j])
        for i in range(count) for j in range(2)
    ]
    if first:
        cot_buf = refs[6]
        cot_buf[...] = jnp.zeros_like(cot_buf)
        part, patches = cots[0].shape[1:]
        for f in range(frames):
            for k in range(shards):
                at = pl.multiple_of((place_ref[0] ^ k) * part, part)
                cot_buf[pl.ds(at, part), :patches] = cots[k][f]
            cot = cot_buf[...].T[:step]
            cot_ref[f] = cot
            grad_ref[f * step : (f + 1) * step] = (cot.astype(F32) * scale_ref[f]).astype(LOW)
    for i in range(count):
        up, down = 2 * i, 2 * i + 1
        wait_all(loads[up : down + 1])
        bias = packs[i][0:1]

        def one(f, total, i=i, up=up, down=down, bias=bias):
            at = pl.ds(pl.multiple_of(f * step, step), step)
            pre = mat_mul(mlp_in_ref[at], w_buf[up]) + bias
            sig = 0.5 + 0.5 * jnp.tanh(0.851 * pre)
            act = (pre * sig).astype(LOW)
            act_buf[at] = act
            grad_act = mat_nt(grad_ref[at], w_buf[down])
            grad_pre = (grad_act * (sig + 1.702 * pre * sig * (1.0 - sig))).astype(LOW)
            pre_buf[at] = grad_pre
            out = mat_mul(act, w_buf[down])
            back = mat_nt(grad_pre, w_buf[up])
            if i > 0:
                acc_ref[at] += out
                gacc_ref[at] += back
            elif first:
                acc_ref[at] = out
                gacc_ref[at] = back
            else:
                acc_ref[at] = acc_in[at] + out
                gacc_ref[at] = gacc_in[at] + back
            return total + jnp.sum(grad_pre.astype(F32), axis=0, keepdims=True)

        sums_ref[i] = lax.fori_loop(0, frames, one, jnp.zeros((1, hidden), F32))
        for c in range(0, width, 256):
            g_buf[up, c : c + 256] = mat_tn(mlp_in_ref[:, c : c + 256], pre_buf[...]).astype(LOW)
        stores[up].start()
        for c in range(0, hidden, 256):
            g_buf[down, c : c + 256] = mat_tn(act_buf[:, c : c + 256], grad_ref[...]).astype(LOW)
        stores[down].start()
    for store in stores:
        store.wait()


def mlp_step(frames, place, scale, mlp_in, packs, weights, cots=None, carried=None, after=()):
    rows, width = mlp_in.shape
    count = len(packs)
    first = cots is not None
    hidden = packs[0].shape[1]
    step = rows // frames
    ins = [place, scale, mlp_in, *packs, *(cots if first else carried)]
    shapes = [shaped((frames, step, width), LOW), shaped((rows, width), LOW)] if first else []
    shapes += [shaped((rows, width), F32)] * 2 + [shaped((count, 1, hidden), F32)]
    grads = [shaped((width + hidden, width), LOW)] * count
    scratch = [
        pltpu.VMEM((2 * count, width, hidden), LOW),
        pltpu.VMEM((2 * count, width, hidden), LOW),
        pltpu.VMEM((rows, hidden), LOW),
        pltpu.VMEM((rows, hidden), LOW),
        pltpu.SemaphoreType.DMA((2 * count, 2)),
        pltpu.SemaphoreType.DMA((2 * count,)),
    ]
    if first:
        scratch.append(pltpu.VMEM((width, -(-step // 128) * 128), LOW))
    return call(
        functools.partial(mlp_kernel, frames, count, first, len(after)),
        "mlp",
        in_specs=[SMEM, SMEM, VMEM] + [VMEM] * (len(ins) - 3) + [ANY] * (len(weights) + len(after)),
        out_specs=[VMEM] * len(shapes) + [ANY] * len(grads),
        out_shape=shapes + grads,
        scratch_shapes=scratch,
    )(*ins, *weights, *after)


def attn_backward_kernel(
    shards, waits, place_ref, scale_ref, gain_ref, mlp_gain_ref, res_ref, acc_ref, gacc_ref, mlp_normed_ref, mlp_inv_ref, cot_ref,
    normed_ref, inv_ref, heads_ref, prob_ref, *refs
):
    packs, refs = refs[:shards], refs[shards:]
    ups, refs = refs[: shards // 2], refs[shards // 2 :]
    outs = 2 * shards + 3 + 2
    weights, refs = refs[: len(refs) - outs - waits], refs[len(refs) - outs :]
    toks, grad_toks, refs = refs[:shards], refs[shards : 2 * shards], refs[2 * shards :]
    proj_ref, low_ref, sums_ref, w_buf, w_sem = refs
    part = heads_ref.shape[4]
    patches = toks[0].shape[2]
    seq_pad, width = res_ref.shape[1:]
    gain, mlp_gain = row_of(gain_ref), row_of(mlp_gain_ref)
    frame = pl.program_id(0)
    wide_idx = place_ref[0]
    copies = weight_copies(weights, shards, place_ref, w_buf, w_sem)

    @pl.when(frame == 0)
    def _():
        start_all(copies)
        sums_ref[...] = jnp.zeros_like(sums_ref)
        rows = [ref[i] for ref in ups for i in range(2)]
        for k, values in enumerate(reorder(rows, wide_idx)):
            sums_ref[6 + k] = values

    def columns(values, out_refs):
        blocks = values.T
        blocks = reorder([blocks[j * part : (j + 1) * part, :patches] for j in range(shards)], wide_idx)
        for ref, block in zip(out_refs, blocks):
            ref[0] = block

    down_bias = jnp.concatenate(reorder([p[1:2, 3 * part : 4 * part] for p in packs], wide_idx), axis=1)
    columns((res_ref[0] + acc_ref[0] + down_bias).astype(LOW), toks)
    grad_res = cot_ref[0].astype(F32) * scale_ref[frame]
    gacc, mlp_normed = gacc_ref[0], mlp_normed_ref[0]
    hidden = grad_res + norm_back(gacc, mlp_normed, mlp_inv_ref[0], mlp_gain)

    def add_sum(row, values):
        sums_ref[row] += jnp.sum(values, axis=0, keepdims=True)

    add_sum(0, grad_res)
    add_sum(1, gacc * mlp_normed)
    add_sum(2, gacc)
    add_sum(3, hidden)
    low = hidden.astype(LOW)
    low_ref[0] = low
    masks = head_masks(part)
    scale = HD ** (-0.5)
    back = jnp.zeros(hidden.shape, F32)
    bias_sums = []

    @pl.when(frame == 0)
    def _():
        wait_all(copies)

    for k in range(shards):
        grad_mix = mat_nt(low, w_buf[k, 3 * part :]).astype(LOW)
        queries, keys, values = heads_ref[0, k, 0], heads_ref[0, k, 1], heads_ref[0, k, 2]
        prob_low = prob_ref[0, k]
        prob = prob_low.astype(F32)
        mix_heads = stack_heads(grad_mix, masks)
        grad_value = mat_tn(prob_low, mix_heads)
        grad_prob = mat_nt(mix_heads, values)
        grad_score = (
            prob * (grad_prob - jnp.sum(prob * grad_prob, axis=-1, keepdims=True))
        ).astype(LOW)
        grad_query = pick_heads(mat_mul(grad_score, keys), masks)
        grad_key = mat_tn(grad_score, stack_heads(queries, masks))
        proj = jnp.concatenate([grad_query * scale, grad_key * scale, grad_value], axis=1).astype(LOW)
        proj_ref[0, k] = proj
        bias_sums.append(jnp.sum(proj.astype(F32), axis=0, keepdims=True))
        back += mat_mul(proj, w_buf[k, : 3 * part])
    for i, at in ((6 + shards, 0), (7 + shards, 2 * part)):
        own = reorder([values[:, at : at + part] for values in bias_sums], wide_idx)
        sums_ref[i] += jnp.concatenate(own, axis=1)
    normed = normed_ref[0]
    add_sum(4, back * normed)
    add_sum(5, back)
    total = hidden + norm_back(back, normed, inv_ref[0], gain)
    row = lax.broadcasted_iota(jnp.int32, (seq_pad, 1), 0)
    sums_ref[8 + shards + frame] = jnp.sum(jnp.where(row == patches, total, 0.0), axis=0, keepdims=True)
    columns(total.astype(LOW), grad_toks)


def attn_backward(patches, place, scale, vecs, per_frame, packs, ups, weights, after):
    frames, seq_pad, width = per_frame[0].shape
    heads = per_frame[8]
    shards, part = heads.shape[1], heads.shape[4]
    blocks = [(frames, part, patches)] * (2 * shards)
    proj = (frames, shards, seq_pad, 3 * part)
    return call(
        functools.partial(attn_backward_kernel, shards, len(after)),
        "attn_backward",
        grid=(frames,),
        in_specs=[SMEM, SMEM]
        + [whole(v) for v in vecs]
        + [per_step(v.shape) for v in per_frame]
        + [whole(v) for v in list(packs) + list(ups)]
        + [ANY] * (len(weights) + len(after)),
        out_specs=[per_step(b) for b in blocks]
        + [per_step(proj), per_step((frames, seq_pad, width)), fixed((8 + shards + frames, 1, width))],
        out_shape=[shaped(b, LOW) for b in blocks]
        + [
            shaped(proj, LOW),
            shaped((frames, seq_pad, width), LOW),
            shaped((8 + shards + frames, 1, width), F32),
        ],
        scratch_shapes=[
            pltpu.VMEM((shards, 4 * part, width), LOW),
            pltpu.SemaphoreType.DMA((shards, 2)),
        ],
    )(place, scale, *vecs, *per_frame, *packs, *ups, *weights, *after)


def attn_grads_kernel(waits, attn_in_ref, low_ref, proj_ref, mix_ref, *refs):
    grad_refs, (proj_buf, mix_buf) = refs[waits:-2], refs[-2:]
    count = len(grad_refs)
    frames, seq_pad, part = mix_ref.shape[0], mix_ref.shape[2], mix_ref.shape[3]
    for i in range(count):
        for f in range(frames):
            at = slice(f * seq_pad, (f + 1) * seq_pad)
            proj_buf[at] = proj_ref[f, i]
            mix_buf[at] = mix_ref[f, i]
        for c in range(0, 3 * part, part):
            grad_refs[i][c : c + part] = mat_tn(proj_buf[:, c : c + part], attn_in_ref[...]).astype(LOW)
        grad_refs[i][3 * part :] = mat_tn(mix_buf[...], low_ref[...]).astype(LOW)


def attn_grads(attn_in, proj, low, mix, pair, after):
    frames, shards, seq_pad, part = mix.shape
    width = attn_in.shape[-1]
    rows = frames * seq_pad
    count = min(2, shards)

    def shard(array):
        return pl.BlockSpec((frames, count) + array.shape[2:], lambda i: (0, pair, 0, 0))

    return call(
        functools.partial(attn_grads_kernel, len(after)),
        "attn_grads",
        grid=(1,),
        in_specs=[fixed((rows, width)), fixed((rows, width)), shard(proj), shard(mix)] + [ANY] * len(after),
        out_specs=[fixed((4 * part, width))] * count,
        out_shape=[shaped((4 * part, width), LOW)] * count,
        scratch_shapes=[pltpu.VMEM((rows, 3 * part), LOW), pltpu.VMEM((rows, part), LOW)],
    )(attn_in.reshape(rows, width), low.reshape(rows, width), proj, mix, *after)


def same_video(place_ref, group, rows, columns):
    first = pl.program_id(0) * columns

    def video(position):
        position = position + first
        return (((position // group) ^ place_ref[2]) * group + position % group) // VIDEO_FRAMES

    row = lax.broadcasted_iota(jnp.int32, (rows, columns), 0) % columns
    column = lax.broadcasted_iota(jnp.int32, (rows, columns), 1)
    return video(row) == video(column)


def message_forward_kernel(
    group, waits, place_ref, cls_ref, weight_ref, m_bias_ref, gain_ref, shift_ref, offset_ref, flat_ref, bias_ref,
    proj_ref, *refs
):
    normed_ref, inv_ref, in_ref, heads_ref, prob_ref, mix_ref, base_ref, sum_ref = refs[waits:]
    part = proj_ref.shape[0]
    chunk = cls_ref.shape[0]
    message = mat_mul(cls_ref[...], weight_ref[...]) + row_of(m_bias_ref)
    normed, inv = normalize(message)
    normed_ref[...] = normed
    inv_ref[...] = inv
    msg_in = (normed * row_of(gain_ref) + row_of(shift_ref)).astype(LOW)
    in_ref[...] = msg_in
    proj = mat_nt(msg_in, flat_ref[...])
    queries = (proj[:, :part] + bias_ref[0:1]).astype(LOW)
    keys = proj[:, part : 2 * part].astype(LOW)
    values = (proj[:, 2 * part :] + bias_ref[1:2]).astype(LOW)
    heads_ref[0, 0] = queries
    heads_ref[0, 1] = keys
    heads_ref[0, 2] = values
    masks = head_masks(part)
    scores = mat_nt(stack_heads(queries, masks, HD ** (-0.5)), keys)
    scores = jnp.where(same_video(place_ref, group, len(masks) * chunk, chunk), scores, -1e30)
    exps = jnp.exp(scores - jnp.max(scores, axis=-1, keepdims=True))
    prob = exps / jnp.sum(exps, axis=-1, keepdims=True)
    prob_ref[0] = prob
    mix = pick_heads(mat_mul(prob.astype(LOW), values), masks).astype(LOW)
    mix_ref[...] = mix

    @pl.when(pl.program_id(0) == 0)
    def _():
        base_ref[...] = message[:group] + row_of(offset_ref)
        sum_ref[...] = mat_mul(mix, proj_ref[...])[:group]


def message_forward(chunk, group, place, cls_rows, weight, vecs, flat, bias, proj, after):
    count, width = cls_rows.shape
    part = proj.shape[0]
    heads = part // HD
    chunks = count // chunk
    rows = lambda columns: pl.BlockSpec((chunk, columns), lambda c: (c, 0))
    return call(
        functools.partial(message_forward_kernel, group, len(after)),
        "message_forward",
        grid=(chunks,),
        in_specs=[SMEM, rows(width)]
        + [whole(v) for v in (weight, *vecs, flat, bias, proj)]
        + [ANY] * len(after),
        out_specs=[
            rows(width), rows(1), rows(width),
            per_step((chunks, 3, chunk, part)), per_step((chunks, heads * chunk, chunk)),
            rows(part), fixed((group, width)), fixed((group, width)),
        ],
        out_shape=[
            shaped((count, width), F32),
            shaped((count, 1), F32),
            shaped((count, width), LOW),
            shaped((chunks, 3, chunk, part), LOW),
            shaped((chunks, heads * chunk, chunk), F32),
            shaped((count, part), LOW),
            shaped((group, width), F32),
            shaped((group, width), F32),
        ],
    )(place, cls_rows, weight, *vecs, flat, bias, proj, *after)


def message_backward_kernel(
    waits, grad_ref, in_ref, heads_ref, prob_ref, mix_ref, flat_ref, proj_ref, *refs
):
    grad_flat_ref, grad_proj_ref, sum_grad_ref, sum_cross_ref, back_ref = refs[waits:]

    @pl.when(pl.program_id(0) == 0)
    def _():
        for ref in (grad_flat_ref, grad_proj_ref, sum_grad_ref, sum_cross_ref):
            ref[...] = jnp.zeros_like(ref)

    part = proj_ref.shape[0]
    masks = head_masks(part)
    grad = grad_ref[:, 0].astype(LOW)
    sum_grad_ref[...] += jnp.sum(grad.astype(F32), axis=0, keepdims=True)
    grad_proj_ref[...] += mat_tn(mix_ref[...], grad)
    grad_mix = mat_nt(grad, proj_ref[...]).astype(LOW)
    mix_heads = stack_heads(grad_mix, masks)
    queries, keys, values = heads_ref[0, 0], heads_ref[0, 1], heads_ref[0, 2]
    prob = prob_ref[0]
    grad_prob = mat_nt(mix_heads, values)
    grad_score = prob * (grad_prob - jnp.sum(prob * grad_prob, axis=-1, keepdims=True))
    score_low = grad_score.astype(LOW)
    grad_query = pick_heads(mat_mul(score_low, keys), masks) * HD ** (-0.5)
    grad_key = mat_tn(score_low, stack_heads(queries, masks)) * HD ** (-0.5)
    grad_value = mat_tn(prob.astype(LOW), mix_heads)
    cross = jnp.concatenate([grad_query, grad_key, grad_value], axis=1).astype(LOW)
    sum_cross_ref[...] += jnp.sum(cross.astype(F32), axis=0, keepdims=True)
    grad_flat_ref[...] += mat_tn(cross, in_ref[...])
    back_ref[...] = mat_mul(cross, flat_ref[...])


def message_backward(grad, msg_in, heads, prob, mix, flat, proj, after):
    count, _, width = grad.shape
    part = proj.shape[0]
    chunks, _, chunk, _ = heads.shape
    rows = lambda columns: pl.BlockSpec((chunk, columns), lambda c: (c, 0))
    shapes = [(3 * part, width), (part, width), (1, width), (1, 3 * part)]
    return call(
        functools.partial(message_backward_kernel, len(after)),
        "message_backward",
        grid=(chunks,),
        in_specs=[
            pl.BlockSpec((chunk, 1, width), lambda c: (c, 0, 0)),
            rows(width), per_step(heads.shape), per_step(prob.shape), rows(part), whole(flat), whole(proj),
        ]
        + [ANY] * len(after),
        out_specs=[fixed(s) for s in shapes] + [rows(width)],
        out_shape=[shaped(s, F32) for s in shapes + [(count, width)]],
    )(grad, msg_in, heads, prob, mix, flat, proj, *after)


def message_end_kernel(
    group, passed, grad_ref, back_ref, other_ref, normed_ref, inv_ref, gain_ref, cls_ref, weight_ref, *refs
):
    grad_weight_ref, sums_ref, grad_cls_ref = refs[passed : passed + 3]

    @pl.when(pl.program_id(0) == 0)
    def _():
        grad_weight_ref[...] = jnp.zeros_like(grad_weight_ref)
        sums_ref[...] = jnp.zeros_like(sums_ref)

    back = back_ref[...] + other_ref[...].astype(F32)
    normed = normed_ref[...]
    grad = grad_ref[:, 0] + norm_back(back, normed, inv_ref[...], row_of(gain_ref))
    low = grad.astype(LOW)
    for row, values in enumerate((low.astype(F32), back * normed, back)):
        sums_ref[row : row + 1] += jnp.sum(values, axis=0, keepdims=True)
    grad_weight_ref[...] += mat_tn(cls_ref[...], low)

    @pl.when(pl.program_id(0) == 0)
    def _():
        grad_cls_ref[...] = mat_nt(weight_ref[...], low)[:, :group]


def message_end(chunk, group, grad, back, other, normed, inv, gain, cls_rows, weight, passed):
    count, _, width = grad.shape
    rows = lambda columns: pl.BlockSpec((chunk, columns), lambda c: (c, 0))
    return call(
        functools.partial(message_end_kernel, group, len(passed)),
        "message_end",
        grid=(count // chunk,),
        in_specs=[pl.BlockSpec((chunk, 1, width), lambda c: (c, 0, 0))] + [rows(width)] * 3 + [rows(1), whole(gain), rows(width), whole(weight)]
        + [ANY] * len(passed),
        out_specs=[fixed((width, width)), fixed((8, width)), fixed((width, group))] + [ANY] * len(passed),
        out_shape=[shaped((width, width), F32), shaped((8, width), F32), shaped((width, group), F32)]
        + [shaped(v.shape, v.dtype) for v in passed],
        input_output_aliases={8 + i: 3 + i for i in range(len(passed))},
    )(grad, back, other, normed, inv, gain, cls_rows, weight, *passed)


def gate_kernel(*refs):
    pass


def gate(arrays, after, micros=0.0):
    count = len(arrays)
    return call(
        gate_kernel,
        "gate",
        micros,
        in_specs=[ANY] * (count + len(after)),
        out_specs=[ANY] * count,
        out_shape=[shaped(v.shape, v.dtype) for v in arrays],
        input_output_aliases={i: i for i in range(count)},
    )(*arrays, *after)


def merge_kernel(count, ordered, place_ref, *refs):
    refs, out_ref = refs[:-1], refs[-1]
    size = refs[0].shape[0] - count
    total = refs[0][:count]
    for ref in refs[1:]:
        total += ref[:count]
    out_ref[:count] = total
    for k, ref in enumerate(refs):
        at = (place_ref[0] ^ k) if ordered else k
        out_ref[pl.ds(count + at * size, size)] = ref[count:]


def merge(place, count, buffers, ordered=False):
    rows, one, width = buffers[0].shape
    return call(
        functools.partial(merge_kernel, count, ordered),
        "merge",
        in_specs=[SMEM] + [VMEM] * len(buffers),
        out_specs=VMEM,
        out_shape=shaped((count + (rows - count) * len(buffers), one, width), F32),
    )(place, *buffers)


def collect_kernel(place_ref, *refs):
    *pieces, grad_cls_ref, out_ref = refs
    frames, part, patches = pieces[0].shape
    own = grad_cls_ref[pl.ds(pl.multiple_of(place_ref[0] * part, part), part), :]
    lane = lax.broadcasted_iota(jnp.int32, (part, patches), 1)
    for j, piece in enumerate(reorder([ref[...] for ref in pieces], place_ref[0])):
        for f in range(frames):
            i = j * frames + f
            out_ref[i] = jnp.where(lane == 0, piece[f].astype(F32) + own[:, i : i + 1], piece[f].astype(F32)).astype(LOW)


def collect(place, pieces, grad_cls):
    frames, part, patches = pieces[0].shape
    shape = (frames * len(pieces), part, patches)
    return call(
        collect_kernel,
        "collect",
        in_specs=[SMEM] + [VMEM] * (len(pieces) + 1),
        out_specs=VMEM,
        out_shape=shaped(shape, LOW),
    )(place, *pieces, grad_cls)


def swap(block, axis, flip):
    return lax.ppermute(block, axis, [(i, i ^ flip) for i in range(lax.axis_size(axis))])


def nothing(array):
    one = lax.slice(array, (0,) * array.ndim, (1,) * array.ndim).reshape(()).astype(F32)
    return one * 0.0


def zero_of(array):
    return nothing(array).astype(jnp.int32)


def frames_in(block, after):
    count = lax.axis_size("wide")
    index = lax.axis_index("wide")
    part = block.shape[0] // count
    begin = zero_of(after)
    pieces = [lax.dynamic_slice_in_dim(block, (index ^ k) * part + begin, part, 0) for k in range(count)]
    return [piece if k == 0 else swap(piece, "wide", k) for k, piece in enumerate(pieces)]


def send_half(block, after):
    odd = lax.axis_index("narrow") & 1
    half = block.shape[0] // 2
    sent = lax.dynamic_slice_in_dim(block, odd * half + zero_of(after), half, 0)
    return [swap(sent, "wide", bit) for bit in bits_of(lax.axis_size("wide"))[1:]]


def near_shards(block):
    return [block, swap(block, "wide", 1)]


def far_shards(near, far):
    return [near, far, swap(near, "wide", 1), swap(far, "wide", 1)]


def added(terms, start, size):
    total = sum(
        lax.dynamic_slice_in_dim(array, begin + start, size, 0).astype(F32) for array, begin in terms
    )
    return total.astype(LOW)


def halve(terms, size, bit):
    size = size // 2
    odd = ((lax.axis_index("narrow") & bit) != 0).astype(jnp.int32)
    sent = added(terms, (1 - odd) * size, size)
    received = swap(sent, "narrow", bit)
    return [(array, start + odd * size) for array, start in terms] + [(received, 0)], size, sent, received


def halve_all(terms, size, bits):
    for bit in bits:
        terms, size, _, _ = halve(terms, size, bit)
    return terms, size


def join_all(block, bits):
    for bit in reversed(bits):
        odd = (lax.axis_index("narrow") & bit) != 0
        other = swap(block, "narrow", bit)
        block = jnp.where(
            odd, jnp.concatenate([other, block], axis=0), jnp.concatenate([block, other], axis=0)
        )
    return block


def body(
    frame_tokens,
    cotangent,
    caption_count,
    caption_len,
    message_weight,
    message_bias,
    message_gain,
    message_shift,
    cross_qkv,
    cross_bias,
    cross_proj,
    cross_offset,
    attn_gain,
    attn_shift,
    qkv_weight,
    qkv_bias,
    out_weight,
    out_bias,
    mlp_gain,
    mlp_shift,
    up_weight,
    up_bias,
    down_weight,
    down_bias,
):
    group, patches, part = frame_tokens.shape
    width = message_weight.shape[0]
    hidden = up_weight.shape[1]
    wide = lax.axis_size("wide")
    narrow = lax.axis_size("narrow")
    wide_idx = lax.axis_index("wide")
    narrow_idx = lax.axis_index("narrow")
    frames = group // wide
    seq_pad = -(-(patches + 1) // ROW_TILE) * ROW_TILE
    rows = frames * seq_pad
    all_frames = group * narrow
    chunk = max(c for c in range(VIDEO_FRAMES, 129, VIDEO_FRAMES) if all_frames % c == 0 and c % group == 0)
    place = jnp.stack([wide_idx, narrow_idx & 1, narrow_idx]).astype(jnp.int32)

    def own_cols(values):
        return lax.dynamic_slice_in_dim(values, wide_idx * part, part, values.ndim - 1)

    tokens_t = frame_tokens.transpose(0, 2, 1)
    pack = jnp.concatenate(
        [up_bias, qkv_bias.reshape(-1), out_bias, down_bias, frame_tokens[:, 0, :].astype(F32).reshape(-1)]
    ).reshape(-1, width)
    packs = [pack] + [swap(pack, "wide", k) for k in range(1, wide)]
    cls_rows = jnp.concatenate(
        reorder([p[2:].reshape(group, part).astype(LOW) for p in packs], wide_idx), axis=1
    )
    for bit in bits_of(narrow):
        cls_rows = jnp.concatenate([cls_rows, swap(cls_rows, "narrow", bit)], axis=0)
    toks = frames_in(tokens_t, packs[-1])
    attn_own = jnp.concatenate(
        [qkv_weight.transpose(1, 2, 0).reshape(3 * part, width), out_weight], axis=0
    )
    attn_weights = near_shards(attn_own)
    attn_near = send_half(attn_own, packs[-1])
    attn_far = [swap(near, "narrow", 1) for near in attn_near]
    for near, far in zip(attn_near, attn_far):
        attn_weights += far_shards(near, far)

    cots = frames_in(cotangent.transpose(0, 2, 1), attn_far[0])

    caption_slot = jnp.arange(caption_len.shape[1])
    word_total = jnp.sum(
        jnp.where(caption_slot[None, :] < caption_count[:, None], caption_len, 0), axis=1
    ).astype(F32)
    video_scale = word_total / jnp.mean(word_total)
    own_video = (narrow_idx * group + wide_idx * frames + jnp.arange(frames)) // VIDEO_FRAMES
    video_match = own_video[:, None] == jnp.arange(video_scale.shape[0])[None, :]
    scale = jnp.sum(jnp.where(video_match, video_scale[None, :], 0.0), axis=1)

    cross_flat = cross_qkv.transpose(1, 2, 0).reshape(3 * part, width)
    msg_normed, msg_inv, msg_in, cross_heads, cross_prob, cross_mix, base, group_sum = message_forward(
        chunk, group, place, cls_rows, message_weight,
        (message_bias, message_gain, message_shift, cross_offset), cross_flat, cross_bias, cross_proj,
        attn_far + toks[1:] + cots[1:],
    )
    group_sums = [group_sum] + [swap(group_sum, "wide", k) for k in range(1, wide)]

    odd, begin = narrow_idx & 1, zero_of(group_sums[-1])
    half = width // 2
    mlp_half = jnp.concatenate(
        [lax.dynamic_slice_in_dim(w, odd * half + begin, half, 0) for w in (up_weight, down_weight)], axis=0
    )
    mlp_near = [swap(mlp_half, "wide", bit) for bit in bits_of(wide)[1:]]
    up_shards, down_shards = near_shards(up_weight), near_shards(down_weight)

    (normed, inv, attn_in, heads, prob, mix, hidden_res, mlp_normed, mlp_inv, mlp_in) = attn_forward(
        seq_pad, place, (attn_gain, attn_shift, mlp_gain, mlp_shift), base, toks, group_sums, packs, attn_weights,
        [up_shards[1], down_shards[1]],
    )
    mlp_in = mlp_in.reshape(rows, width)
    bits = bits_of(narrow)
    size = width + hidden
    mlp_near = gate(mlp_near, [mlp_in])
    cot, grad_rows, acc, gacc, sum_up, *grad_own = mlp_step(
        frames, place, scale, mlp_in, packs[:2], up_shards + down_shards, cots=cots, after=mlp_near
    )
    *mlp_far, grad_next = gate([swap(near, "narrow", 1) for near in mlp_near] + [grad_own[1]], [acc])
    own_terms = [(grad_own[0], 0), (swap(grad_next, "wide", 1), 0)]
    own_terms, own_size, own_sent, own_received = halve(own_terms, size, bits[0])
    mlp_weights = [piece for near, far in zip(mlp_near, mlp_far) for piece in far_shards(near, far)]
    acc, gacc, sum_up_far, *grad_far = mlp_step(
        frames, place, scale, mlp_in, packs[2:], mlp_weights, carried=(grad_rows, acc, gacc), after=[own_sent]
    )
    grad_far = gate(grad_far, [own_received])
    own_terms, own_size, own_sent, own_next = halve(own_terms, own_size, bits[1])
    far_terms = [(grad_far[0], 0), (swap(grad_far[1], "wide", 1), 0)]
    far_terms, far_size, far_sent, far_received = halve(far_terms, size, bits[0])

    shape = (frames, seq_pad, width)
    per_frame = (
        hidden_res, acc.reshape(shape), gacc.reshape(shape), mlp_normed, mlp_inv, cot, normed, inv, heads, prob
    )
    *blocks, proj, low, sums = attn_backward(
        patches, place, scale, (attn_gain, mlp_gain), per_frame, packs, [sum_up, sum_up_far], attn_weights,
        [own_sent, far_sent],
    )
    grad_attn = list(attn_grads(attn_in, proj, low, mix, 1, [far_received, own_next]))
    half = 2 * part
    attn_far = [(grad_attn[0], 0), (swap(grad_attn[1], "wide", 1), 0)]
    attn_sent = added(attn_far, 0, 2 * half)
    attn_received = swap(attn_sent, "wide", 2)
    grad_attn = gate(attn_grads(attn_in, proj, low, mix, 0, [attn_sent]), [attn_received])
    attn_own = [(grad_attn[0], 0), (swap(grad_attn[1], "wide", 1), 0)]

    own_terms, own_size = halve_all(own_terms, own_size, bits[2:])
    far_terms, far_size = halve_all(far_terms, far_size, bits[1:])
    crossed = swap(added(far_terms, 0, far_size), "wide", 2)
    grad_mlp = join_all(added(own_terms + [(crossed, 0)], 0, own_size), bits).astype(F32)
    grad_attn_own = []
    for at in (0, half):
        terms, left = halve_all([(array, at) for array, _ in attn_own + [(attn_received, 0)]], half, bits)
        grad_attn_own.append(join_all(added(terms, 0, left), bits))
    grad_attn_own = jnp.concatenate(grad_attn_own, axis=0).astype(F32)

    (sums,) = gate([sums], [far_received, own_next])
    count = 8 + wide
    sums = merge(place, count, [sums] + [swap(sums, "wide", k) for k in range(1, wide)], True)
    for bit in bits:
        sums = merge(place, count, [sums, swap(sums, "narrow", bit)])
    grad_msg = sums[count:]
    sums = sums[:count].reshape(count, width)
    grad_up_bias = lax.dynamic_slice_in_dim(sums[6 : 6 + wide].reshape(-1), wide_idx * hidden, hidden, 0)

    grad_cross_flat, grad_cross_proj, sum_cross_grad, sum_cross, back = message_backward(
        grad_msg, msg_in, cross_heads, cross_prob, cross_mix, cross_flat, cross_proj, [attn_received]
    )
    bits = bits_of(wide)
    for bit in bits[:-1]:
        back = back + swap(back, "wide", bit)
    grad_message_weight, msg_sums, grad_cls, *blocks = message_end(
        chunk, group, grad_msg, back, swap(back.astype(LOW), "wide", bits[-1]), msg_normed, msg_inv, message_gain, cls_rows,
        message_weight, blocks,
    )

    def frames_out(pieces):
        return [piece if k == 0 else swap(piece, "wide", k) for k, piece in enumerate(pieces)]

    out_pieces = frames_out(blocks[:wide])
    grad_pieces = frames_out(blocks[wide:])
    output_tokens = jnp.concatenate(reorder(out_pieces, wide_idx), axis=0)
    grad_tokens = collect(place, grad_pieces, grad_cls)

    return (
        output_tokens.transpose(0, 2, 1),
        grad_tokens.transpose(0, 2, 1),
        grad_message_weight,
        msg_sums[0],
        msg_sums[1],
        msg_sums[2],
        grad_cross_flat.reshape(3, part, width).transpose(2, 0, 1),
        jnp.stack([sum_cross[0, :part], sum_cross[0, 2 * part :]]),
        grad_cross_proj,
        sum_cross_grad[0],
        sums[4],
        sums[5],
        grad_attn_own[: 3 * part].reshape(3, part, width).transpose(2, 0, 1),
        own_cols(sums[count - 2 :]),
        grad_attn_own[3 * part :],
        own_cols(sums[3]),
        sums[1],
        sums[2],
        grad_mlp[:width],
        grad_up_bias,
        grad_mlp[width:],
        own_cols(sums[0]),
    )


def solution(mesh):
    return jax.shard_map(
        body,
        mesh=mesh,
        in_specs=(
            P("narrow", None, "wide"),
            P("narrow", None, "wide"),
            P(),
            P(),
            P(),
            P(),
            P(),
            P(),
            P(None, None, "wide"),
            P(None, "wide"),
            P("wide", None),
            P(),
            P(),
            P(),
            P(None, None, "wide"),
            P(None, "wide"),
            P("wide", None),
            P("wide"),
            P(),
            P(),
            P(None, "wide"),
            P("wide"),
            P("wide", None),
            P("wide"),
        ),
        out_specs=(
            P("narrow", None, "wide"),
            P("narrow", None, "wide"),
            P(),
            P(),
            P(),
            P(),
            P(None, None, "wide"),
            P(None, "wide"),
            P("wide", None),
            P(),
            P(),
            P(),
            P(None, None, "wide"),
            P(None, "wide"),
            P("wide", None),
            P("wide"),
            P(),
            P(),
            P(None, "wide"),
            P("wide"),
            P("wide", None),
            P("wide"),
        ),
        check_vma=False,
    )
```

profile of v0, /device:TPU:0, one launch (start us, length us, event | category | flops | bytes accessed | tf_op | source)
XLA Modules:
  0.0 440.1 jit_solution(14404492717419164869)
XLA Ops:
  2.3 2.4 collective-permute-start
  4.7 1.6 collective-permute-done.refs_11_.refs_1_.refs_3_
  8.2 2.5 collective-permute-start.6
  10.8 14.1 %collective-permute-done.1.refs_10_.refs_0_.refs_2_ = f32[5,768]{1,0:T(8,128)S(1)} collective-permute-done((f32[5,768]{1,0:T(8,128)S(1)}, f32[5,768]{1,0:T(8,128)S(1)}, u32[]{:S(2)}, u32[]{:S(2)}) %collective-permute-start.1) | collective-permute-done | bytes 15392 | tf_op jit(solution)/shard_map/ppermute | solution.py:748
  25.2 1.8 collective-permute-start.7
  28.3 12.4 %collective-permute-done.3 = bf16[12,768]{1,0:T(8,128)(2,1)} collective-permute-done((bf16[12,768]{1,0:T(8,128)(2,1)}, bf16[12,768]{1,0:T(8,128)(2,1)}, u32[]{:S(2)}, u32[]{:S(2)}) %collective-permute-start.3) | collective-permute-done | bytes 18464 | tf_op jit(solution)/shard_map/ppermute | solution.py:748
  43.1 2.3 dynamic-slice_bitcast_fusion.1
  48.7 2.7 collective-permute-start.5
  52.6 2.0 dynamic-slice_bitcast_fusion
  61.0 7.1 %collective-permute-done.12.refs_5_.refs_4_ = bf16[3,192,197]{2,1,0:T(8,128)(2,1)S(1)} collective-permute-done((bf16[3,192,197]{2,1,0:T(8,128)(2,1)S(1)}, bf16[3,192,197]{2,1,0:T(8,128)(2,1)S(1)}, u32[]{:S(2)}, u32[]{:S(2)}) %collective-permute-start.12) | collective-permute-done | bytes 226976 | tf_op jit(solution)/shard_map/ppermute | solution.py:748
  68.1 5.4 %collective-permute-done.13.refs_6_.refs_5_ = bf16[3,192,197]{2,1,0:T(8,128)(2,1)S(1)} collective-permute-done((bf16[3,192,197]{2,1,0:T(8,128)(2,1)S(1)}, bf16[3,192,197]{2,1,0:T(8,128)(2,1)S(1)}, u32[]{:S(2)}, u32[]{:S(2)}) %collective-permute-start.13) | collective-permute-done | bytes 226976 | tf_op jit(solution)/shard_map/ppermute | solution.py:748
  74.3 4.1 message_forward.1
  80.3 1.9 collective-permute-done.16.refs_7_
  85.6 1.6 collective-permute-start.22
  90.1 24.7 %collective-permute-done.15.refs_6_ = f32[12,768]{1,0:T(8,128)S(1)} collective-permute-done((f32[12,768]{1,0:T(8,128)S(1)}, f32[12,768]{1,0:T(8,128)S(1)}, u32[]{:S(2)}, u32[]{:S(2)}) %collective-permute-start.15) | collective-permute-done | bytes 36896 | tf_op jit(solution)/shard_map/ppermute | solution.py:748
  115.6 22.5 %attn_forward.1 = (f32[3,208,768]{2,1,0:T(8,128)}, f32[3,208,1]{2,1,0:T(8,128)}, bf16[3,208,768]{2,1,0:T(8,128)(2,1)}, bf16[3,4,3,208,192]{4,3,2,1,0:T(8,128)(2,...) custom-call(s32[3]{0:T(128)} %pad_add_fusion.place_ref, ...), custom_call_target="tpu_custom_call" | custom-call | tf_op jit(solution)/shard_map/attn_forward/pallas_call | solution.py:233
  142.7 19.2 %mlp.2 = (bf16[3,208,768]{2,1,0:T(8,128)(2,1)}, bf16[624,768]{1,0:T(8,128)(2,1)}, f32[624,768]{1,0:T(8,128)}, f32[624,768]{1,0:T(8,128)}, f32[2,1,768]{2,1,0:T(1...) custom-call(s32[3]{0:T(128)} %pad_add_fusion.place_ref, f32[3]{0:T(128)} %select_reduce_fusion.1.scale_ref, ...), custom_call_target="tpu_custom_call" | custom-call | tf_op jit(solution)/shard_map/mlp/pallas_call | solution.py:357
  161.9 4.8 %collective-permute-done.23.refs_0_ = bf16[768,768]{1,0:T(8,128)(2,1)S(1)} collective-permute-done((bf16[768,768]{1,0:T(8,128)(2,1)}, bf16[768,768]{1,0:T(8,128)(2,1)S(1)}, u32[]{:S(2)}, u32[]{:S(2)}) %collective-permute-start.23) | collective-permute-done | bytes 1179680 | tf_op jit(solution)/shard_map/ppermute | solution.py:748
  169.5 3.0 collective-permute-done.26
  172.5 2.4 add_convert_fusion.2.refs_9_
  174.9 1.6 collective-permute-start.27
  177.9 19.9 %mlp.3 = (f32[624,768]{1,0:T(8,128)}, f32[624,768]{1,0:T(8,128)}, f32[2,1,768]{2,1,0:T(1,128)}, bf16[1536,768]{1,0:T(8,128)(2,1)}, bf16[1536,768]{1,0:T(8,128)(2,1)}) custom-call(s32[3]{0:T(128)} %pad_add_fusion.place_ref, f32[3]{0:T(128)} %select_reduce_fusion.1.scale_ref, bf16[624,768]{1,0:T(8,128)(2,1)} %bitcast.63, f32[5,768]{1,0:T(8,128)} %copy-done.44, ...), custom_call_target="tpu_custom_call" | custom-call | tf_op jit(solution)/shard_map/mlp/pallas_call | solution.py:357
  197.8 5.2 %collective-permute-done.27.refs_2_ = bf16[768,768]{1,0:T(8,128)(2,1)S(1)} collective-permute-done((bf16[768,768]{1,0:T(8,128)(2,1)S(1)}, bf16[768,768]{1,0:T(8,128)(2,1)S(1)}, u32[]{:S(2)}, u32[]{:S(2)}) %collective-permute-start.27) | collective-permute-done | bytes 1179680 | tf_op jit(solution)/shard_map/ppermute | solution.py:748
  204.0 4.7 %collective-permute-done.28 = bf16[1536,768]{1,0:T(8,128)(2,1)S(1)} collective-permute-done((bf16[1536,768]{1,0:T(8,128)(2,1)}, bf16[1536,768]{1,0:T(8,128)(2,1)S(1)}, u32[]{:S(2)}, u32[]{:S(2)}) %collective-permute-start.28) | collective-permute-done | bytes 2359328 | tf_op jit(solution)/shard_map/ppermute | solution.py:748
  208.8 2.5 add_convert_fusion.1.refs_13_
  211.3 1.6 collective-permute-start.29
  215.2 24.1 %attn_backward.1 = (bf16[3,192,197]{2,1,0:T(8,128)(2,1)}, bf16[3,192,197]{2,1,0:T(8,128)(2,1)}, bf16[3,192,197]{2,1,0:T(8,128)(2,1)}, bf16[3,192,197]{2,1,0:T(8,...) custom-call(s32[3]{0:T(128)} %pad_add_fusion.place_ref, ...), custom_call_target="tpu_custom_call" | custom-call | tf_op jit(solution)/shard_map/attn_backward/pallas_call | solution.py:458
  240.5 5.5 %attn_grads.2 = (bf16[768,768]{1,0:T(8,128)(2,1)}, bf16[768,768]{1,0:T(8,128)(2,1)}) custom-call(bf16[624,768]{1,0:T(8,128)(2,1)} %bitcast.64, bf16[624,768]{1,0:T(8,128)(2,1)} %bitcast.66, bf16[3,4,208,576]{3,2,1,0:T(8,128)(2,1)} %get-tuple-element.122.proj_ref, bf16[3,4,208,192]{3,2,1,0:T(8,128)(2,1)} %get-tuple-element.123.mix_ref, ...), custom_call_target="tpu_custom_call" | custom-call | tf_op jit(solution)/shard_map/attn_grads/pallas_call | solution.py:505
  246.0 2.5 add_convert_fusion.3
  252.7 11.8 %collective-permute-done.61 = bf16[384,768]{1,0:T(8,128)(2,1)S(1)} collective-permute-done((bf16[384,768]{1,0:T(8,128)(2,1)}, bf16[384,768]{1,0:T(8,128)(2,1)S(1)}, u32[]{:S(2)}, u32[]{:S(2)}) %collective-permute-start.61) | collective-permute-done | bytes 589856 | tf_op jit(solution)/shard_map/ppermute | solution.py:748
  264.4 1.9 add_convert_fusion.7
  266.3 2.6 collective-permute-start.62
  270.6 19.0 %collective-permute-done.62 = bf16[192,768]{1,0:T(8,128)(2,1)} collective-permute-done((bf16[192,768]{1,0:T(8,128)(2,1)}, bf16[192,768]{1,0:T(8,128)(2,1)}, u32[]{:S(2)}, u32[]{:S(2)}) %collective-permute-start.62) | collective-permute-done | bytes 294944 | tf_op jit(solution)/shard_map/ppermute | solution.py:748
  292.5 5.5 %attn_grads.3 = (bf16[768,768]{1,0:T(8,128)(2,1)}, bf16[768,768]{1,0:T(8,128)(2,1)}) custom-call(bf16[624,768]{1,0:T(8,128)(2,1)} %bitcast.65, bf16[624,768]{1,0:T(8,128)(2,1)} %bitcast.67, bf16[3,4,208,576]{3,2,1,0:T(8,128)(2,1)} %get-tuple-element.122.proj_ref, bf16[3,4,208,192]{3,2,1,0:T(8,128)(2,1)} %get-tuple-element.123.mix_ref, ...), custom_call_target="tpu_custom_call" | custom-call | tf_op jit(solution)/shard_map/attn_grads/pallas_call | solution.py:505
  302.4 3.3 collective-permute-done.32.refs_2_
  309.5 3.5 collective-permute-done.34.refs_1_
  315.2 3.5 collective-permute-start.35
  318.7 3.1 collective-permute-done.35.refs_1_
  322.5 1.7 merge.6.refs_0_
  326.4 8.4 %collective-permute-done.36.refs_1_ = f32[60,1,768]{2,1,0:T(1,128)S(1)} collective-permute-done((f32[60,1,768]{2,1,0:T(1,128)}, f32[60,1,768]{2,1,0:T(1,128)S(1)}, u32[]{:S(2)}, u32[]{:S(2)}) %collective-permute-start.36) | collective-permute-done | bytes 184352 | tf_op jit(solution)/shard_map/ppermute | solution.py:748
  335.5 1.8 merge.7
  337.3 1.7 slice.131.grad_ref
  344.3 4.7 %message_backward.1 = (f32[576,768]{1,0:T(8,128)}, f32[192,768]{1,0:T(8,128)}, f32[1,768]{1,0:T(1,128)}, f32[1,576]{1,0:T(1,128)}, f32[96,768]{1,0:T(8,128)}) custom-call(f32[96,1,768]{2,1,0:T(1,128)} %slice.131.grad_ref, bf16[96,768]{1,0:T(8,128)(2,1)} %get-tuple-element.116.in_ref, bf16[1,3,96,192]{3,2,1,0:T(8,128)(2,1)} %get-tuple-element.117.heads_ref, ...), custom_call_target="tpu_custom_call" | custom-call | tf_op jit(solution)/shard_map/message_backward/pallas_call | solution.py:631
  350.4 2.0 collective-permute-start.54
  353.3 7.0 %collective-permute-done.48 = bf16[192,768]{1,0:T(8,128)(2,1)S(1)} collective-permute-done((bf16[192,768]{1,0:T(8,128)(2,1)S(1)}, bf16[192,768]{1,0:T(8,128)(2,1)S(1)}, u32[]{:S(2)}, u32[]{:S(2)}) %collective-permute-start.48) | collective-permute-done | bytes 294944 | tf_op jit(solution)/shard_map/ppermute | solution.py:748
  360.2 5.9 %collective-permute-done.54 = bf16[192,768]{1,0:T(8,128)(2,1)S(1)} collective-permute-done((bf16[192,768]{1,0:T(8,128)(2,1)S(1)}, bf16[192,768]{1,0:T(8,128)(2,1)S(1)}, u32[]{:S(2)}, u32[]{:S(2)}) %collective-permute-start.54) | collective-permute-done | bytes 294944 | tf_op jit(solution)/shard_map/ppermute | solution.py:748
  366.9 1.8 add_convert_fusion.12
  369.9 4.0 message_end.1
  378.0 1.6 add_convert_fusion.16
  379.5 3.9 collective-permute-done.41
  384.4 5.2 %collective-permute-done.42 = bf16[3,192,197]{2,1,0:T(8,128)(2,1)S(1)} collective-permute-done((bf16[3,192,197]{2,1,0:T(8,128)(2,1)}, bf16[3,192,197]{2,1,0:T(8,128)(2,1)S(1)}, u32[]{:S(2)}, u32[]{:S(2)}) %collective-permute-start.42) | collective-permute-done | bytes 226976 | tf_op jit(solution)/shard_map/ppermute | solution.py:748
  391.2 1.7 collective-permute-start.50
  394.1 1.8 collective-permute-done.45.refs_2_
  395.9 6.4 %collective-permute-done.46.refs_3_ = bf16[3,192,197]{2,1,0:T(8,128)(2,1)S(1)} collective-permute-done((bf16[3,192,197]{2,1,0:T(8,128)(2,1)}, bf16[3,192,197]{2,1,0:T(8,128)(2,1)S(1)}, u32[]{:S(2)}, u32[]{:S(2)}) %collective-permute-start.46) | collective-permute-done | bytes 226976 | tf_op jit(solution)/shard_map/ppermute | solution.py:748
  403.0 2.8 collect.1
  407.0 2.3 collective-permute-start.56
  411.2 3.7 collective-permute-done.56
  416.0 2.2 collective-permute-done.51
  419.5 2.6 collective-permute-done.57
  423.1 2.0 collective-permute-done.52
  425.6 1.7 collective-permute-done.58
  427.4 2.5 fusion.3
  429.9 4.2 collective-permute-done.53
  434.4 3.0 collective-permute-done.59
  (308 shorter events, 88.9 us)
Async XLA Ops:
  2.3 4.0 collective-permute-start
  8.2 17.0 %collective-permute-start.6 = (bf16[384,768]{1,0:T(8,128)(2,1)S(1)}, bf16[384,768]{1,0:T(8,128)(2,1)S(1)}, u32[]{:S(2)}, u32[]{:S(2)}) collective-permute-start(bf16[384,768]{1,0:T(8,128)(2,1)S(1)} %fusion.1), channel_id=1, source_target_pairs={{0,2},{1,3},{2,0},{3,1},{4,6},{5,7},{6,4},{7,5},{8,10},{9,11},{10,... | collective-permute-start | bytes 1769480 | tf_op jit(solution)/shard_map/ppermute | solution.py:748
  10.7 14.1 %collective-permute-start.1 = (f32[5,768]{1,0:T(8,128)S(1)}, f32[5,768]{1,0:T(8,128)S(1)}, u32[]{:S(2)}, u32[]{:S(2)}) collective-permute-start(f32[5,768]{1,0:T(8,128)S(1)} %reshape.160.refs_8_.refs_0_), channel_id=1, source_target_pairs={{0,2},{1,3},{2,0},{3,1},{4,6},{5,7},{6,4},{7,5},{8,10},{9,11},{10,... | collective-permute-start | bytes 46088 | tf_op jit(solution)/shard_map/ppermute | solution.py:748
  10.8 14.2 %collective-permute-start.2 = (f32[5,768]{1,0:T(8,128)S(1)}, f32[5,768]{1,0:T(8,128)S(1)}, u32[]{:S(2)}, u32[]{:S(2)}) collective-permute-start(f32[5,768]{1,0:T(8,128)S(1)} %reshape.160.refs_8_.refs_0_), channel_id=1, source_target_pairs={{0,1},{1,0},{2,3},{3,2},{4,5},{5,4},{6,7},{7,6},{8,9},{9,8},{10,11... | collective-permute-start | bytes 46088 | tf_op jit(solution)/shard_map/ppermute | solution.py:748
  25.2 23.5 %collective-permute-start.7 = (bf16[384,768]{1,0:T(8,128)(2,1)S(1)}, bf16[384,768]{1,0:T(8,128)(2,1)S(1)}, u32[]{:S(2)}, u32[]{:S(2)}) collective-permute-start(bf16[384,768]{1,0:T(8,128)(2,1)S(1)} %collective-permute-done.6.refs_14_.refs_8_), channel_id=1, source_target_pairs={{0,4},{4,0},{8,12},{12,8},{16,20},{20,16},{24,28},{28,24},{1,5},{5... | collective-permute-start | bytes 1769480 | tf_op jit(solution)/shard_map/ppermute | solution.py:748
  27.8 13.0 %collective-permute-start.3 = (bf16[12,768]{1,0:T(8,128)(2,1)}, bf16[12,768]{1,0:T(8,128)(2,1)}, u32[]{:S(2)}, u32[]{:S(2)}) collective-permute-start(bf16[12,768]{1,0:T(8,128)(2,1)} %pad_maximum_fusion.5), channel_id=1, source_target_pairs={{0,4},{4,0},{8,12},{12,8},{16,20},{20,16},{24,28},{28,24},{1,5},{5... | collective-permute-start | bytes 55304 | tf_op jit(solution)/shard_map/ppermute | solution.py:748
  28.2 58.9 %collective-permute-start.17 = (bf16[768,768]{1,0:T(8,128)(2,1)S(1)}, bf16[768,768]{1,0:T(8,128)(2,1)S(1)}, u32[]{:S(2)}, u32[]{:S(2)}) collective-permute-start(bf16[768,768]{1,0:T(8,128)(2,1)S(1)} %pad_maximum_fusion.refs_12_.refs_6_), channel_id=1, source_target_pairs={{0,1},{1,0},{2,3},{3,2},{4,5},{5,4},{6,7},{7,6},{8,9},{9,8},{10,11... | collective-permute-start | bytes 3538952 | tf_op jit(solution)/shard_map/ppermute | solution.py:748
  41.6 5.4 %collective-permute-start.4 = (bf16[24,768]{1,0:T(8,128)(2,1)S(1)}, bf16[24,768]{1,0:T(8,128)(2,1)S(1)}, u32[]{:S(2)}, u32[]{:S(2)}) collective-permute-start(bf16[24,768]{1,0:T(8,128)(2,1)S(1)} %pad_maximum_fusion.4), channel_id=1, source_target_pairs={{0,8},{4,12},{8,0},{12,4},{16,24},{20,28},{24,16},{28,20},{1,9},{5... | collective-permute-start | bytes 110600 | tf_op jit(solution)/shard_map/ppermute | solution.py:748
  45.4 10.6 %collective-permute-start.8 = (bf16[3,192,197]{2,1,0:T(8,128)(2,1)}, bf16[3,192,197]{2,1,0:T(8,128)(2,1)}, u32[]{:S(2)}, u32[]{:S(2)}) collective-permute-start(bf16[3,192,197]{2,1,0:T(8,128)(2,1)} %get-tuple-element.183), channel_id=1, source_target_pairs={{0,1},{1,0},{2,3},{3,2},{4,5},{5,4},{6,7},{7,6},{8,9},{9,8},{10,11... | collective-permute-start | bytes 680840 | tf_op jit(solution)/shard_map/ppermute | solution.py:748
  45.4 12.1 %collective-permute-start.9 = (bf16[3,192,197]{2,1,0:T(8,128)(2,1)}, bf16[3,192,197]{2,1,0:T(8,128)(2,1)}, u32[]{:S(2)}, u32[]{:S(2)}) collective-permute-start(bf16[3,192,197]{2,1,0:T(8,128)(2,1)} %get-tuple-element.182), channel_id=1, source_target_pairs={{0,2},{1,3},{2,0},{3,1},{4,6},{5,7},{6,4},{7,5},{8,10},{9,11},{10,... | collective-permute-start | bytes 680840 | tf_op jit(solution)/shard_map/ppermute | solution.py:748
  47.0 14.0 %collective-permute-start.10 = (bf16[3,192,197]{2,1,0:T(8,128)(2,1)}, bf16[3,192,197]{2,1,0:T(8,128)(2,1)}, u32[]{:S(2)}, u32[]{:S(2)}) collective-permute-start(bf16[3,192,197]{2,1,0:T(8,128)(2,1)} %get-tuple-element.184), channel_id=1, source_target_pairs={{0,3},{1,2},{2,1},{3,0},{4,7},{5,6},{6,5},{7,4},{8,11},{9,10},{10,... | collective-permute-start | bytes 680840 | tf_op jit(solution)/shard_map/ppermute | solution.py:748
  48.7 7.3 %collective-permute-start.5 = (bf16[48,768]{1,0:T(8,128)(2,1)}, bf16[48,768]{1,0:T(8,128)(2,1)S(1)}, u32[]{:S(2)}, u32[]{:S(2)}) collective-permute-start(bf16[48,768]{1,0:T(8,128)(2,1)} %pad_maximum_fusion.3), channel_id=1, source_target_pairs={{0,16},{4,20},{8,24},{12,28},{16,0},{20,4},{24,8},{28,12},{1,17},{... | collective-permute-start | bytes 221192 | tf_op jit(solution)/shard_map/ppermute | solution.py:748
  56.0 5.0 %collective-permute-start.11 = (bf16[3,192,197]{2,1,0:T(8,128)(2,1)S(1)}, bf16[3,192,197]{2,1,0:T(8,128)(2,1)S(1)}, u32[]{:S(2)}, u32[]{:S(2)}) collective-permute-start(bf16[3,192,197]{2,1,0:T(8,128)(2,1)S(1)} %get-tuple-element.179), channel_id=1, source_target_pairs={{0,1},{1,0},{2,3},{3,2},{4,5},{5,4},{6,7},{7,6},{8,9},{9,8},{10,11... | collective-permute-start | bytes 680840 | tf_op jit(solution)/shard_map/ppermute | solution.py:748
  56.0 12.1 %collective-permute-start.12 = (bf16[3,192,197]{2,1,0:T(8,128)(2,1)S(1)}, bf16[3,192,197]{2,1,0:T(8,128)(2,1)S(1)}, u32[]{:S(2)}, u32[]{:S(2)}) collective-permute-start(bf16[3,192,197]{2,1,0:T(8,128)(2,1)S(1)} %get-tuple-element.178), channel_id=1, source_target_pairs={{0,2},{1,3},{2,0},{3,1},{4,6},{5,7},{6,4},{7,5},{8,10},{9,11},{10,... | collective-permute-start | bytes 680840 | tf_op jit(solution)/shard_map/ppermute | solution.py:748
  57.5 16.0 %collective-permute-start.13 = (bf16[3,192,197]{2,1,0:T(8,128)(2,1)S(1)}, bf16[3,192,197]{2,1,0:T(8,128)(2,1)S(1)}, u32[]{:S(2)}, u32[]{:S(2)}) collective-permute-start(bf16[3,192,197]{2,1,0:T(8,128)(2,1)S(1)} %get-tuple-element.180), channel_id=1, source_target_pairs={{0,3},{1,2},{2,1},{3,0},{4,7},{5,6},{6,5},{7,4},{8,11},{9,10},{10,... | collective-permute-start | bytes 680840 | tf_op jit(solution)/shard_map/ppermute | solution.py:748
  78.4 3.9 collective-permute-start.16
  79.8 7.9 %collective-permute-start.20 = (bf16[768,768]{1,0:T(8,128)(2,1)S(1)}, bf16[768,768]{1,0:T(8,128)(2,1)}, u32[]{:S(2)}, u32[]{:S(2)}) collective-permute-start(bf16[768,768]{1,0:T(8,128)(2,1)S(1)} %copy-done.19), channel_id=1, source_target_pairs={{0,1},{1,0},{2,3},{3,2},{4,5},{5,4},{6,7},{7,6},{8,9},{9,8},{10,11... | collective-permute-start | bytes 3538952 | tf_op jit(solution)/shard_map/ppermute | solution.py:748
  80.1 7.8 %collective-permute-start.21 = (bf16[768,768]{1,0:T(8,128)(2,1)}, bf16[768,768]{1,0:T(8,128)(2,1)}, u32[]{:S(2)}, u32[]{:S(2)}) collective-permute-start(bf16[768,768]{1,0:T(8,128)(2,1)} %refs_8_.1), channel_id=1, source_target_pairs={{0,1},{1,0},{2,3},{3,2},{4,5},{5,4},{6,7},{7,6},{8,9},{9,8},{10,11... | collective-permute-start | bytes 3538952 | tf_op jit(solution)/shard_map/ppermute | solution.py:748
  85.6 52.6 %collective-permute-start.22 = (bf16[768,768]{1,0:T(8,128)(2,1)S(1)}, bf16[768,768]{1,0:T(8,128)(2,1)S(1)}, u32[]{:S(2)}, u32[]{:S(2)}) collective-permute-start(bf16[768,768]{1,0:T(8,128)(2,1)S(1)} %pad_maximum_fusion.1), channel_id=1, source_target_pairs={{0,2},{1,3},{2,0},{3,1},{4,6},{5,7},{6,4},{7,5},{8,10},{9,11},{10,... | collective-permute-start | bytes 3538952 | tf_op jit(solution)/shard_map/ppermute | solution.py:748
  87.2 27.6 %collective-permute-start.19 = (bf16[384,768]{1,0:T(8,128)(2,1)S(1)}, bf16[384,768]{1,0:T(8,128)(2,1)S(1)}, u32[]{:S(2)}, u32[]{:S(2)}) collective-permute-start(bf16[384,768]{1,0:T(8,128)(2,1)S(1)} %copy-done.8), channel_id=1, source_target_pairs={{0,1},{1,0},{2,3},{3,2},{4,5},{5,4},{6,7},{7,6},{8,9},{9,8},{10,11... | collective-permute-start | bytes 1769480 | tf_op jit(solution)/shard_map/ppermute | solution.py:748
  87.8 26.9 %collective-permute-start.15 = (f32[12,768]{1,0:T(8,128)S(1)}, f32[12,768]{1,0:T(8,128)S(1)}, u32[]{:S(2)}, u32[]{:S(2)}) collective-permute-start(f32[12,768]{1,0:T(8,128)S(1)} %copy-done.58), channel_id=1, source_target_pairs={{0,2},{1,3},{2,0},{3,1},{4,6},{5,7},{6,4},{7,5},{8,10},{9,11},{10,... | collective-permute-start | bytes 110600 | tf_op jit(solution)/shard_map/ppermute | solution.py:748
  139.2 27.5 %collective-permute-start.23 = (bf16[768,768]{1,0:T(8,128)(2,1)}, bf16[768,768]{1,0:T(8,128)(2,1)S(1)}, u32[]{:S(2)}, u32[]{:S(2)}) collective-permute-start(bf16[768,768]{1,0:T(8,128)(2,1)} %gate.5.refs_10_.refs_5_), channel_id=1, source_target_pairs={{0,4},{4,0},{8,12},{12,8},{16,20},{20,16},{24,28},{28,24},{1,5},{5... | collective-permute-start | bytes 3538952 | tf_op jit(solution)/shard_map/ppermute | solution.py:748
  167.8 4.7 %collective-permute-start.26 = (bf16[1536,768]{1,0:T(8,128)(2,1)}, bf16[1536,768]{1,0:T(8,128)(2,1)S(1)}, u32[]{:S(2)}, u32[]{:S(2)}) collective-permute-start(bf16[1536,768]{1,0:T(8,128)(2,1)} %get-tuple-element.99), channel_id=1, source_target_pairs={{0,1},{1,0},{2,3},{3,2},{4,5},{5,4},{6,7},{7,6},{8,9},{9,8},{10,11... | collective-permute-start | bytes 7077896 | tf_op jit(solution)/shard_map/ppermute | solution.py:748
  169.0 7.5 %collective-permute-start.24 = (bf16[768,768]{1,0:T(8,128)(2,1)S(1)}, bf16[768,768]{1,0:T(8,128)(2,1)S(1)}, u32[]{:S(2)}, u32[]{:S(2)}) collective-permute-start(bf16[768,768]{1,0:T(8,128)(2,1)S(1)} %copy-done.1), channel_id=1, source_target_pairs={{0,1},{1,0},{2,3},{3,2},{4,5},{5,4},{6,7},{7,6},{8,9},{9,8},{10,11... | collective-permute-start | bytes 3538952 | tf_op jit(solution)/shard_map/ppermute | solution.py:748
  169.0 7.5 %collective-permute-start.25 = (bf16[768,768]{1,0:T(8,128)(2,1)}, bf16[768,768]{1,0:T(8,128)(2,1)S(1)}, u32[]{:S(2)}, u32[]{:S(2)}) collective-permute-start(bf16[768,768]{1,0:T(8,128)(2,1)} %get-tuple-element.97.refs_6_), channel_id=1, source_target_pairs={{0,1},{1,0},{2,3},{3,2},{4,5},{5,4},{6,7},{7,6},{8,9},{9,8},{10,11... | collective-permute-start | bytes 3538952 | tf_op jit(solution)/shard_map/ppermute | solution.py:748
  174.9 28.1 %collective-permute-start.27 = (bf16[768,768]{1,0:T(8,128)(2,1)S(1)}, bf16[768,768]{1,0:T(8,128)(2,1)S(1)}, u32[]{:S(2)}, u32[]{:S(2)}) collective-permute-start(bf16[768,768]{1,0:T(8,128)(2,1)S(1)} %add_convert_fusion.2.refs_9_), channel_id=1, source_target_pairs={{0,4},{4,0},{8,12},{12,8},{16,20},{20,16},{24,28},{28,24},{1,5},{5... | collective-permute-start | bytes 3538952 | tf_op jit(solution)/shard_map/ppermute | solution.py:748
  204.0 4.7 %collective-permute-start.28 = (bf16[1536,768]{1,0:T(8,128)(2,1)}, bf16[1536,768]{1,0:T(8,128)(2,1)S(1)}, u32[]{:S(2)}, u32[]{:S(2)}) collective-permute-start(bf16[1536,768]{1,0:T(8,128)(2,1)} %get-tuple-element.114), channel_id=1, source_target_pairs={{0,1},{1,0},{2,3},{3,2},{4,5},{5,4},{6,7},{7,6},{8,9},{9,8},{10,11... | collective-permute-start | bytes 7077896 | tf_op jit(solution)/shard_map/ppermute | solution.py:748
  211.3 28.1 %collective-permute-start.29 = (bf16[768,768]{1,0:T(8,128)(2,1)S(1)}, bf16[768,768]{1,0:T(8,128)(2,1)S(1)}, u32[]{:S(2)}, u32[]{:S(2)}) collective-permute-start(bf16[768,768]{1,0:T(8,128)(2,1)S(1)} %add_convert_fusion.1.refs_13_), channel_id=1, source_target_pairs={{0,4},{4,0},{8,12},{12,8},{16,20},{20,16},{24,28},{28,24},{1,5},{5... | collective-permute-start | bytes 3538952 | tf_op jit(solution)/shard_map/ppermute | solution.py:748
  214.4 24.9 %collective-permute-start.30 = (bf16[384,768]{1,0:T(8,128)(2,1)S(1)}, bf16[384,768]{1,0:T(8,128)(2,1)S(1)}, u32[]{:S(2)}, u32[]{:S(2)}) collective-permute-start(bf16[384,768]{1,0:T(8,128)(2,1)S(1)} %add_convert_fusion.4.refs_12_), channel_id=1, source_target_pairs={{0,8},{4,12},{8,0},{12,4},{16,24},{20,28},{24,16},{28,20},{1,9},{5... | collective-permute-start | bytes 1769480 | tf_op jit(solution)/shard_map/ppermute | solution.py:748
  246.0 3.8 collective-permute-start.37
  248.5 15.9 %collective-permute-start.61 = (bf16[384,768]{1,0:T(8,128)(2,1)}, bf16[384,768]{1,0:T(8,128)(2,1)S(1)}, u32[]{:S(2)}, u32[]{:S(2)}) collective-permute-start(bf16[384,768]{1,0:T(8,128)(2,1)} %add_convert_fusion.3), channel_id=1, source_target_pairs={{0,8},{4,12},{8,0},{12,4},{16,24},{20,28},{24,16},{28,20},{1,9},{5... | collective-permute-start | bytes 1769480 | tf_op jit(solution)/shard_map/ppermute | solution.py:748
  251.1 46.8 %collective-permute-start.38 = (bf16[768,768]{1,0:T(8,128)(2,1)}, bf16[768,768]{1,0:T(8,128)(2,1)S(1)}, u32[]{:S(2)}, u32[]{:S(2)}) collective-permute-start(bf16[768,768]{1,0:T(8,128)(2,1)} %add_convert_fusion.refs_0_), channel_id=1, source_target_pairs={{0,2},{1,3},{2,0},{3,1},{4,6},{5,7},{6,4},{7,5},{8,10},{9,11},{10,... | collective-permute-start | bytes 3538952 | tf_op jit(solution)/shard_map/ppermute | solution.py:748
  266.3 23.3 %collective-permute-start.62 = (bf16[192,768]{1,0:T(8,128)(2,1)}, bf16[192,768]{1,0:T(8,128)(2,1)}, u32[]{:S(2)}, u32[]{:S(2)}) collective-permute-start(bf16[192,768]{1,0:T(8,128)(2,1)} %add_convert_fusion.7), channel_id=1, source_target_pairs={{0,16},{4,20},{8,24},{12,28},{16,0},{20,4},{24,8},{28,12},{1,17},{... | collective-permute-start | bytes 884744 | tf_op jit(solution)/shard_map/ppermute | solution.py:748
  270.2 28.8 %collective-permute-start.60 = (bf16[192,768]{1,0:T(8,128)(2,1)S(1)}, bf16[192,768]{1,0:T(8,128)(2,1)S(1)}, u32[]{:S(2)}, u32[]{:S(2)}) collective-permute-start(bf16[192,768]{1,0:T(8,128)(2,1)S(1)} %add_convert_fusion.8), channel_id=1, source_target_pairs={{0,16},{4,20},{8,24},{12,28},{16,0},{20,4},{24,8},{28,12},{1,17},{... | collective-permute-start | bytes 884744 | tf_op jit(solution)/shard_map/ppermute | solution.py:748
  290.9 8.1 %collective-permute-start.63 = (bf16[192,768]{1,0:T(8,128)(2,1)S(1)}, bf16[192,768]{1,0:T(8,128)(2,1)S(1)}, u32[]{:S(2)}, u32[]{:S(2)}) collective-permute-start(bf16[192,768]{1,0:T(8,128)(2,1)S(1)} %add_convert_fusion.6), channel_id=1, source_target_pairs={{0,2},{1,3},{2,0},{3,1},{4,6},{5,7},{6,4},{7,5},{8,10},{9,11},{10,... | collective-permute-start | bytes 884744 | tf_op jit(solution)/shard_map/ppermute | solution.py:748
  299.0 50.0 %collective-permute-start.47 = (bf16[768,768]{1,0:T(8,128)(2,1)}, bf16[768,768]{1,0:T(8,128)(2,1)}, u32[]{:S(2)}, u32[]{:S(2)}) collective-permute-start(bf16[768,768]{1,0:T(8,128)(2,1)} %get-tuple-element.155), channel_id=1, source_target_pairs={{0,1},{1,0},{2,3},{3,2},{4,5},{5,4},{6,7},{7,6},{8,9},{9,8},{10,11... | collective-permute-start | bytes 3538952 | tf_op jit(solution)/shard_map/ppermute | solution.py:748
  300.4 24.8 %collective-permute-start.64 = (bf16[192,768]{1,0:T(8,128)(2,1)S(1)}, bf16[192,768]{1,0:T(8,128)(2,1)S(1)}, u32[]{:S(2)}, u32[]{:S(2)}) collective-permute-start(bf16[192,768]{1,0:T(8,128)(2,1)S(1)} %add_convert_fusion.5), channel_id=1, source_target_pairs={{0,16},{4,20},{8,24},{12,28},{16,0},{20,4},{24,8},{28,12},{1,17},{... | collective-permute-start | bytes 884744 | tf_op jit(solution)/shard_map/ppermute | solution.py:748
  301.0 4.7 %collective-permute-start.32 = (f32[15,1,768]{2,1,0:T(1,128)}, f32[15,1,768]{2,1,0:T(1,128)S(1)}, u32[]{:S(2)}, u32[]{:S(2)}) collective-permute-start(f32[15,1,768]{2,1,0:T(1,128)} %gate.8.refs_0_), channel_id=1, source_target_pairs={{0,2},{1,3},{2,0},{3,1},{4,6},{5,7},{6,4},{7,5},{8,10},{9,11},{10,... | collective-permute-start | bytes 138248 | tf_op jit(solution)/shard_map/ppermute | solution.py:748
  301.5 4.2 collective-permute-start.33
  308.5 4.6 %collective-permute-start.34 = (f32[24,1,768]{2,1,0:T(1,128)}, f32[24,1,768]{2,1,0:T(1,128)S(1)}, u32[]{:S(2)}, u32[]{:S(2)}) collective-permute-start(f32[24,1,768]{2,1,0:T(1,128)} %merge.4.refs_0_), channel_id=1, source_target_pairs={{0,4},{4,0},{8,12},{12,8},{16,20},{20,16},{24,28},{28,24},{1,5},{5... | collective-permute-start | bytes 221192 | tf_op jit(solution)/shard_map/ppermute | solution.py:748
  315.2 6.6 %collective-permute-start.35 = (f32[36,1,768]{2,1,0:T(1,128)}, f32[36,1,768]{2,1,0:T(1,128)S(1)}, u32[]{:S(2)}, u32[]{:S(2)}) collective-permute-start(f32[36,1,768]{2,1,0:T(1,128)} %merge.5.refs_0_), channel_id=1, source_target_pairs={{0,8},{4,12},{8,0},{12,4},{16,24},{20,28},{24,16},{28,20},{1,9},{5... | collective-permute-start | bytes 331784 | tf_op jit(solution)/shard_map/ppermute | solution.py:748
  324.1 10.7 %collective-permute-start.36 = (f32[60,1,768]{2,1,0:T(1,128)}, f32[60,1,768]{2,1,0:T(1,128)S(1)}, u32[]{:S(2)}, u32[]{:S(2)}) collective-permute-start(f32[60,1,768]{2,1,0:T(1,128)} %merge.6.refs_0_), channel_id=1, source_target_pairs={{0,16},{4,20},{8,24},{12,28},{16,0},{20,4},{24,8},{28,12},{1,17},{... | collective-permute-start | bytes 552968 | tf_op jit(solution)/shard_map/ppermute | solution.py:748
  325.3 18.5 %collective-permute-start.65 = (bf16[384,768]{1,0:T(8,128)(2,1)S(1)}, bf16[384,768]{1,0:T(8,128)(2,1)S(1)}, u32[]{:S(2)}, u32[]{:S(2)}) collective-permute-start(bf16[384,768]{1,0:T(8,128)(2,1)S(1)} %maximum_select_fusion.4), channel_id=1, source_target_pairs={{0,8},{4,12},{8,0},{12,4},{16,24},{20,28},{24,16},{28,20},{1,9},{5... | collective-permute-start | bytes 1769480 | tf_op jit(solution)/shard_map/ppermute | solution.py:748
  349.0 3.5 collective-permute-start.39
  350.3 9.9 %collective-permute-start.48 = (bf16[192,768]{1,0:T(8,128)(2,1)S(1)}, bf16[192,768]{1,0:T(8,128)(2,1)S(1)}, u32[]{:S(2)}, u32[]{:S(2)}) collective-permute-start(bf16[192,768]{1,0:T(8,128)(2,1)S(1)} %get-tuple-element.171), channel_id=1, source_target_pairs={{0,4},{4,0},{8,12},{12,8},{16,20},{20,16},{24,28},{28,24},{1,5},{5... | collective-permute-start | bytes 884744 | tf_op jit(solution)/shard_map/ppermute | solution.py:748
  350.4 15.7 %collective-permute-start.54 = (bf16[192,768]{1,0:T(8,128)(2,1)S(1)}, bf16[192,768]{1,0:T(8,128)(2,1)S(1)}, u32[]{:S(2)}, u32[]{:S(2)}) collective-permute-start(bf16[192,768]{1,0:T(8,128)(2,1)S(1)} %get-tuple-element.172), channel_id=1, source_target_pairs={{0,4},{4,0},{8,12},{12,8},{16,20},{20,16},{24,28},{28,24},{1,5},{5... | collective-permute-start | bytes 884744 | tf_op jit(solution)/shard_map/ppermute | solution.py:748
  353.3 16.7 %collective-permute-start.40 = (bf16[96,768]{1,0:T(8,128)(2,1)}, bf16[96,768]{1,0:T(8,128)(2,1)}, u32[]{:S(2)}, u32[]{:S(2)}) collective-permute-start(bf16[96,768]{1,0:T(8,128)(2,1)} %get-tuple-element.163), channel_id=1, source_target_pairs={{0,2},{1,3},{2,0},{3,1},{4,6},{5,7},{6,4},{7,5},{8,10},{9,11},{10,... | collective-permute-start | bytes 442376 | tf_op jit(solution)/shard_map/ppermute | solution.py:748
  368.7 8.6 %collective-permute-start.49 = (bf16[96,768]{1,0:T(8,128)(2,1)}, bf16[96,768]{1,0:T(8,128)(2,1)}, u32[]{:S(2)}, u32[]{:S(2)}) collective-permute-start(bf16[96,768]{1,0:T(8,128)(2,1)} %get-tuple-element.169), channel_id=1, source_target_pairs={{0,8},{4,12},{8,0},{12,4},{16,24},{20,28},{24,16},{28,20},{1,9},{5... | collective-permute-start | bytes 442376 | tf_op jit(solution)/shard_map/ppermute | solution.py:748
  373.9 9.5 %collective-permute-start.41 = (bf16[3,192,197]{2,1,0:T(8,128)(2,1)}, bf16[3,192,197]{2,1,0:T(8,128)(2,1)S(1)}, u32[]{:S(2)}, u32[]{:S(2)}) collective-permute-start(bf16[3,192,197]{2,1,0:T(8,128)(2,1)} %get-tuple-element.137), channel_id=1, source_target_pairs={{0,3},{1,2},{2,1},{3,0},{4,7},{5,6},{6,5},{7,4},{8,11},{9,10},{10,... | collective-permute-start | bytes 680840 | tf_op jit(solution)/shard_map/ppermute | solution.py:748
  374.0 15.6 %collective-permute-start.42 = (bf16[3,192,197]{2,1,0:T(8,128)(2,1)}, bf16[3,192,197]{2,1,0:T(8,128)(2,1)S(1)}, u32[]{:S(2)}, u32[]{:S(2)}) collective-permute-start(bf16[3,192,197]{2,1,0:T(8,128)(2,1)} %get-tuple-element.138), channel_id=1, source_target_pairs={{0,2},{1,3},{2,0},{3,1},{4,6},{5,7},{6,4},{7,5},{8,10},{9,11},{10,... | collective-permute-start | bytes 680840 | tf_op jit(solution)/shard_map/ppermute | solution.py:748
  375.3 15.1 %collective-permute-start.43 = (bf16[3,192,197]{2,1,0:T(8,128)(2,1)}, bf16[3,192,197]{2,1,0:T(8,128)(2,1)S(1)}, u32[]{:S(2)}, u32[]{:S(2)}) collective-permute-start(bf16[3,192,197]{2,1,0:T(8,128)(2,1)} %get-tuple-element.139), channel_id=1, source_target_pairs={{0,1},{1,0},{2,3},{3,2},{4,5},{5,4},{6,7},{7,6},{8,9},{9,8},{10,11... | collective-permute-start | bytes 680840 | tf_op jit(solution)/shard_map/ppermute | solution.py:748
  375.8 15.4 %collective-permute-start.44 = (bf16[3,192,197]{2,1,0:T(8,128)(2,1)}, bf16[3,192,197]{2,1,0:T(8,128)(2,1)S(1)}, u32[]{:S(2)}, u32[]{:S(2)}) collective-permute-start(bf16[3,192,197]{2,1,0:T(8,128)(2,1)} %get-tuple-element.142), channel_id=1, source_target_pairs={{0,1},{1,0},{2,3},{3,2},{4,5},{5,4},{6,7},{7,6},{8,9},{9,8},{10,11... | collective-permute-start | bytes 680840 | tf_op jit(solution)/shard_map/ppermute | solution.py:748
  377.3 45.3 %collective-permute-start.66 = (bf16[768,768]{1,0:T(8,128)(2,1)S(1)}, bf16[768,768]{1,0:T(8,128)(2,1)S(1)}, u32[]{:S(2)}, u32[]{:S(2)}) collective-permute-start(bf16[768,768]{1,0:T(8,128)(2,1)S(1)} %maximum_select_fusion.1), channel_id=1, source_target_pairs={{0,4},{4,0},{8,12},{12,8},{16,20},{20,16},{24,28},{28,24},{1,5},{5... | collective-permute-start | bytes 3538952 | tf_op jit(solution)/shard_map/ppermute | solution.py:748
  383.4 12.4 %collective-permute-start.45 = (bf16[3,192,197]{2,1,0:T(8,128)(2,1)}, bf16[3,192,197]{2,1,0:T(8,128)(2,1)S(1)}, u32[]{:S(2)}, u32[]{:S(2)}) collective-permute-start(bf16[3,192,197]{2,1,0:T(8,128)(2,1)} %get-tuple-element.143), channel_id=1, source_target_pairs={{0,2},{1,3},{2,0},{3,1},{4,6},{5,7},{6,4},{7,5},{8,10},{9,11},{10,... | collective-permute-start | bytes 680840 | tf_op jit(solution)/shard_map/ppermute | solution.py:748
  389.6 12.7 %collective-permute-start.46 = (bf16[3,192,197]{2,1,0:T(8,128)(2,1)}, bf16[3,192,197]{2,1,0:T(8,128)(2,1)S(1)}, u32[]{:S(2)}, u32[]{:S(2)}) collective-permute-start(bf16[3,192,197]{2,1,0:T(8,128)(2,1)} %get-tuple-element.144), channel_id=1, source_target_pairs={{0,3},{1,2},{2,1},{3,0},{4,7},{5,6},{6,5},{7,4},{8,11},{9,10},{10,... | collective-permute-start | bytes 680840 | tf_op jit(solution)/shard_map/ppermute | solution.py:748
  390.4 15.5 %collective-permute-start.55 = (bf16[96,768]{1,0:T(8,128)(2,1)S(1)}, bf16[96,768]{1,0:T(8,128)(2,1)S(1)}, u32[]{:S(2)}, u32[]{:S(2)}) collective-permute-start(bf16[96,768]{1,0:T(8,128)(2,1)S(1)} %copy-done.53), channel_id=1, source_target_pairs={{0,8},{4,12},{8,0},{12,4},{16,24},{20,28},{24,16},{28,20},{1,9},{5... | collective-permute-start | bytes 442376 | tf_op jit(solution)/shard_map/ppermute | solution.py:748
  391.2 14.6 %collective-permute-start.50 = (bf16[48,768]{1,0:T(8,128)(2,1)}, bf16[48,768]{1,0:T(8,128)(2,1)}, u32[]{:S(2)}, u32[]{:S(2)}) collective-permute-start(bf16[48,768]{1,0:T(8,128)(2,1)} %add_convert_fusion.16), channel_id=1, source_target_pairs={{0,16},{4,20},{8,24},{12,28},{16,0},{20,4},{24,8},{28,12},{1,17},{... | collective-permute-start | bytes 221192 | tf_op jit(solution)/shard_map/ppermute | solution.py:748
  407.0 8.0 %collective-permute-start.56 = (bf16[48,768]{1,0:T(8,128)(2,1)S(1)}, bf16[48,768]{1,0:T(8,128)(2,1)S(1)}, u32[]{:S(2)}, u32[]{:S(2)}) collective-permute-start(bf16[48,768]{1,0:T(8,128)(2,1)S(1)} %get-tuple-element.168), channel_id=1, source_target_pairs={{0,16},{4,20},{8,24},{12,28},{16,0},{20,4},{24,8},{28,12},{1,17},{... | collective-permute-start | bytes 221192 | tf_op jit(solution)/shard_map/ppermute | solution.py:748
  410.5 7.6 %collective-permute-start.51 = (bf16[48,768]{1,0:T(8,128)(2,1)S(1)}, bf16[48,768]{1,0:T(8,128)(2,1)S(1)}, u32[]{:S(2)}, u32[]{:S(2)}) collective-permute-start(bf16[48,768]{1,0:T(8,128)(2,1)S(1)} %get-tuple-element.167), channel_id=1, source_target_pairs={{0,16},{4,20},{8,24},{12,28},{16,0},{20,4},{24,8},{28,12},{1,17},{... | collective-permute-start | bytes 221192 | tf_op jit(solution)/shard_map/ppermute | solution.py:748
  415.9 6.2 %collective-permute-start.57 = (bf16[48,768]{1,0:T(8,128)(2,1)S(1)}, bf16[48,768]{1,0:T(8,128)(2,1)S(1)}, u32[]{:S(2)}, u32[]{:S(2)}) collective-permute-start(bf16[48,768]{1,0:T(8,128)(2,1)S(1)} %add_convert_fusion.13), channel_id=1, source_target_pairs={{0,16},{4,20},{8,24},{12,28},{16,0},{20,4},{24,8},{28,12},{1,17},{... | collective-permute-start | bytes 221192 | tf_op jit(solution)/shard_map/ppermute | solution.py:748
  418.2 6.9 %collective-permute-start.52 = (bf16[96,768]{1,0:T(8,128)(2,1)S(1)}, bf16[96,768]{1,0:T(8,128)(2,1)S(1)}, u32[]{:S(2)}, u32[]{:S(2)}) collective-permute-start(bf16[96,768]{1,0:T(8,128)(2,1)S(1)} %maximum_select_fusion.7), channel_id=1, source_target_pairs={{0,8},{4,12},{8,0},{12,4},{16,24},{20,28},{24,16},{28,20},{1,9},{5... | collective-permute-start | bytes 442376 | tf_op jit(solution)/shard_map/ppermute | solution.py:748
  422.1 5.2 %collective-permute-start.58 = (bf16[96,768]{1,0:T(8,128)(2,1)S(1)}, bf16[96,768]{1,0:T(8,128)(2,1)S(1)}, u32[]{:S(2)}, u32[]{:S(2)}) collective-permute-start(bf16[96,768]{1,0:T(8,128)(2,1)S(1)} %maximum_select_fusion.8), channel_id=1, source_target_pairs={{0,8},{4,12},{8,0},{12,4},{16,24},{20,28},{24,16},{28,20},{1,9},{5... | collective-permute-start | bytes 442376 | tf_op jit(solution)/shard_map/ppermute | solution.py:748
  425.1 9.0 %collective-permute-start.53 = (bf16[192,768]{1,0:T(8,128)(2,1)S(1)}, bf16[192,768]{1,0:T(8,128)(2,1)S(1)}, u32[]{:S(2)}, u32[]{:S(2)}) collective-permute-start(bf16[192,768]{1,0:T(8,128)(2,1)S(1)} %maximum_select_fusion.5), channel_id=1, source_target_pairs={{0,4},{4,0},{8,12},{12,8},{16,20},{20,16},{24,28},{28,24},{1,5},{5... | collective-permute-start | bytes 884744 | tf_op jit(solution)/shard_map/ppermute | solution.py:748
  427.4 10.0 %collective-permute-start.59 = (bf16[192,768]{1,0:T(8,128)(2,1)S(1)}, bf16[192,768]{1,0:T(8,128)(2,1)S(1)}, u32[]{:S(2)}, u32[]{:S(2)}) collective-permute-start(bf16[192,768]{1,0:T(8,128)(2,1)S(1)} %maximum_select_fusion.6), channel_id=1, source_target_pairs={{0,4},{4,0},{8,12},{12,8},{16,20},{20,16},{24,28},{28,24},{1,5},{5... | collective-permute-start | bytes 884744 | tf_op jit(solution)/shard_map/ppermute | solution.py:748
  (76 other events, 403.7 us)
where the time goes:
time: 446 us; the launch traced here: 440 us
  waiting for transfers between devices  187 us (42%)
  Pallas kernels  119 us (27%)
  starting transfers between devices  56.3 us (13%)
  other arithmetic  37.3 us (8%)
  local copies, waits for them, and re-layouts  36 us (8%)
    ppermute x67, waiting for transfers between devices, swap(): lax.ppermute(block, axis, [(i, i ^ flip) for i in range(lax.axis_size(axi...  187 us
    ppermute x67, starting transfers between devices, swap(): lax.ppermute(block, axis, [(i, i ^ flip) for i in range(lax.axis_size(axi...  56.3 us
    pallas_call x2, Pallas kernels, mlp_step(): call(functools.partial(mlp_kernel, frames, count, first, len(after)), 'ml...  39.1 us
    pallas_call x1, Pallas kernels, attn_backward(): call(functools.partial(attn_backward_kernel, shards, len(after)), 'attn_b...  24.1 us
    convert_element_type x14, other arithmetic, added(): return total.astype(LOW)  22.9 us
    pallas_call x1, Pallas kernels, attn_forward(): call(functools.partial(attn_forward_kernel, len(after)), 'attn_forward',...  22.5 us
    unnamed x146, local copies, waits for them, and re-layouts  16.2 us
    pallas_call x2, Pallas kernels, attn_grads(): call(functools.partial(attn_grads_kernel, len(after)), 'attn_grads', grid...  10.9 us
  transfers between devices with their start and end apart: 67, of which 34 were waited for; matrix products, arithmetic and copies ran while one was open for 11% of the time, Pallas kernels for 26%

commit v1 on v0

--- a/solution.py
+++ b/solution.py
@@ -233,6 +233,7 @@
     return call(
         functools.partial(attn_forward_kernel, len(after)),
         "attn_forward",
+        23.0,
         grid=(frames,),
         in_specs=[SMEM] + [whole(v) for v in vecs] + [whole(base)]
         + [per_step(v.shape) for v in toks]
@@ -357,6 +358,7 @@
     return call(
         functools.partial(mlp_kernel, frames, count, first, len(after)),
         "mlp",
+        19.5,
         in_specs=[SMEM, SMEM, VMEM] + [VMEM] * (len(ins) - 3) + [ANY] * (len(weights) + len(after)),
         out_specs=[VMEM] * len(shapes) + [ANY] * len(grads),
         out_shape=shapes + grads,
@@ -370,12 +372,12 @@
 ):
     packs, refs = refs[:shards], refs[shards:]
     ups, refs = refs[: shards // 2], refs[shards // 2 :]
-    outs = 2 * shards + 3 + 2
+    outs = shards + 3 + 2
     weights, refs = refs[: len(refs) - outs - waits], refs[len(refs) - outs :]
-    toks, grad_toks, refs = refs[:shards], refs[shards : 2 * shards], refs[2 * shards :]
+    pieces, refs = refs[:shards], refs[shards:]
     proj_ref, low_ref, sums_ref, w_buf, w_sem = refs
     part = heads_ref.shape[4]
-    patches = toks[0].shape[2]
+    patches = pieces[0].shape[3]
     seq_pad, width = res_ref.shape[1:]
     gain, mlp_gain = row_of(gain_ref), row_of(mlp_gain_ref)
     frame = pl.program_id(0)
@@ -390,14 +392,14 @@
         for k, values in enumerate(reorder(rows, wide_idx)):
             sums_ref[6 + k] = values
 
-    def columns(values, out_refs):
+    def columns(values, i):
         blocks = values.T
         blocks = reorder([blocks[j * part : (j + 1) * part, :patches] for j in range(shards)], wide_idx)
-        for ref, block in zip(out_refs, blocks):
-            ref[0] = block
+        for ref, block in zip(pieces, blocks):
+            ref[0, i] = block
 
     down_bias = jnp.concatenate(reorder([p[1:2, 3 * part : 4 * part] for p in packs], wide_idx), axis=1)
-    columns((res_ref[0] + acc_ref[0] + down_bias).astype(LOW), toks)
+    columns((res_ref[0] + acc_ref[0] + down_bias).astype(LOW), 0)
     grad_res = cot_ref[0].astype(F32) * scale_ref[frame]
     gacc, mlp_normed = gacc_ref[0], mlp_normed_ref[0]
     hidden = grad_res + norm_back(gacc, mlp_normed, mlp_inv_ref[0], mlp_gain)
@@ -446,18 +448,19 @@
     total = hidden + norm_back(back, normed, inv_ref[0], gain)
     row = lax.broadcasted_iota(jnp.int32, (seq_pad, 1), 0)
     sums_ref[8 + shards + frame] = jnp.sum(jnp.where(row == patches, total, 0.0), axis=0, keepdims=True)
-    columns(total.astype(LOW), grad_toks)
+    columns(total.astype(LOW), 1)
 
 
 def attn_backward(patches, place, scale, vecs, per_frame, packs, ups, weights, after):
     frames, seq_pad, width = per_frame[0].shape
     heads = per_frame[8]
     shards, part = heads.shape[1], heads.shape[4]
-    blocks = [(frames, part, patches)] * (2 * shards)
+    blocks = [(frames, 2, part, patches)] * shards
     proj = (frames, shards, seq_pad, 3 * part)
     return call(
         functools.partial(attn_backward_kernel, shards, len(after)),
         "attn_backward",
+        24.0,
         grid=(frames,),
         in_specs=[SMEM, SMEM]
         + [whole(v) for v in vecs]
@@ -493,22 +496,18 @@
         grad_refs[i][3 * part :] = mat_tn(mix_buf[...], low_ref[...]).astype(LOW)
 
 
-def attn_grads(attn_in, proj, low, mix, pair, after):
+def attn_grads(attn_in, proj, low, mix, after):
     frames, shards, seq_pad, part = mix.shape
     width = attn_in.shape[-1]
     rows = frames * seq_pad
-    count = min(2, shards)
-
-    def shard(array):
-        return pl.BlockSpec((frames, count) + array.shape[2:], lambda i: (0, pair, 0, 0))
-
     return call(
         functools.partial(attn_grads_kernel, len(after)),
         "attn_grads",
+        0.0,
         grid=(1,),
-        in_specs=[fixed((rows, width)), fixed((rows, width)), shard(proj), shard(mix)] + [ANY] * len(after),
-        out_specs=[fixed((4 * part, width))] * count,
-        out_shape=[shaped((4 * part, width), LOW)] * count,
+        in_specs=[fixed((rows, width)), fixed((rows, width)), fixed(proj.shape), fixed(mix.shape)] + [ANY] * len(after),
+        out_specs=[fixed((4 * part, width))] * shards,
+        out_shape=[shaped((4 * part, width), LOW)] * shards,
         scratch_shapes=[pltpu.VMEM((rows, 3 * part), LOW), pltpu.VMEM((rows, part), LOW)],
     )(attn_in.reshape(rows, width), low.reshape(rows, width), proj, mix, *after)
 
@@ -569,6 +568,7 @@
     return call(
         functools.partial(message_forward_kernel, group, len(after)),
         "message_forward",
+        4.2,
         grid=(chunks,),
         in_specs=[SMEM, rows(width)]
         + [whole(v) for v in (weight, *vecs, flat, bias, proj)]
@@ -592,14 +592,28 @@
 
 
 def message_backward_kernel(
-    waits, grad_ref, in_ref, heads_ref, prob_ref, mix_ref, flat_ref, proj_ref, *refs
+    waits, count, wide, place_ref, all_ref, in_ref, heads_ref, prob_ref, mix_ref, flat_ref, proj_ref, *refs
 ):
-    grad_flat_ref, grad_proj_ref, sum_grad_ref, sum_cross_ref, back_ref = refs[waits:]
-
-    @pl.when(pl.program_id(0) == 0)
+    grad_ref, sums_ref, grad_flat_ref, grad_proj_ref, sum_grad_ref, sum_cross_ref, back_ref = refs[waits:]
+    frames = all_ref.shape[1] - count
+    group = frames * wide
+    step = pl.program_id(0)
+
+    @pl.when(step == 0)
     def _():
         for ref in (grad_flat_ref, grad_proj_ref, sum_grad_ref, sum_cross_ref):
             ref[...] = jnp.zeros_like(ref)
+        total = all_ref[0, :count]
+        for d in range(1, all_ref.shape[0]):
+            total += all_ref[d, :count]
+        sums_ref[...] = total
+
+    groups = grad_ref.shape[0] // group
+    for b in range(groups):
+        holder = ((step * groups + b) ^ place_ref[2]) * wide
+        for w in range(wide):
+            at = b * group + w * frames
+            grad_ref[at : at + frames] = all_ref[holder + w, count:]
 
     part = proj_ref.shape[0]
     masks = head_masks(part)
@@ -622,31 +636,29 @@
     back_ref[...] = mat_mul(cross, flat_ref[...])
 
 
-def message_backward(grad, msg_in, heads, prob, mix, flat, proj, after):
-    count, _, width = grad.shape
+def message_backward(place, count, wide, gathered, msg_in, heads, prob, mix, flat, proj, after):
+    total, width = msg_in.shape
     part = proj.shape[0]
     chunks, _, chunk, _ = heads.shape
     rows = lambda columns: pl.BlockSpec((chunk, columns), lambda c: (c, 0))
-    shapes = [(3 * part, width), (part, width), (1, width), (1, 3 * part)]
+    shapes = [(count, 1, width), (3 * part, width), (part, width), (1, width), (1, 3 * part)]
     return call(
-        functools.partial(message_backward_kernel, len(after)),
+        functools.partial(message_backward_kernel, len(after), count, wide),
         "message_backward",
+        0.0,
         grid=(chunks,),
-        in_specs=[
-            pl.BlockSpec((chunk, 1, width), lambda c: (c, 0, 0)),
-            rows(width), per_step(heads.shape), per_step(prob.shape), rows(part), whole(flat), whole(proj),
-        ]
+        in_specs=[SMEM, whole(gathered), rows(width), per_step(heads.shape), per_step(prob.shape), rows(part)]
+        + [whole(flat), whole(proj)]
         + [ANY] * len(after),
-        out_specs=[fixed(s) for s in shapes] + [rows(width)],
-        out_shape=[shaped(s, F32) for s in shapes + [(count, width)]],
-    )(grad, msg_in, heads, prob, mix, flat, proj, *after)
+        out_specs=[pl.BlockSpec((chunk, 1, width), lambda c: (c, 0, 0))] + [fixed(s) for s in shapes] + [rows(width)],
+        out_shape=[shaped(s, F32) for s in [(total, 1, width)] + shapes + [(total, width)]],
+    )(place, gathered, msg_in, heads, prob, mix, flat, proj, *after)
 
 
 def message_end_kernel(
-    group, passed, grad_ref, back_ref, other_ref, normed_ref, inv_ref, gain_ref, cls_ref, weight_ref, *refs
+    group, grad_ref, back_ref, other_ref, normed_ref, inv_ref, gain_ref, cls_ref, weight_ref, grad_weight_ref,
+    sums_ref, grad_cls_ref
 ):
-    grad_weight_ref, sums_ref, grad_cls_ref = refs[passed : passed + 3]
-
     @pl.when(pl.program_id(0) == 0)
     def _():
         grad_weight_ref[...] = jnp.zeros_like(grad_weight_ref)
@@ -665,20 +677,112 @@
         grad_cls_ref[...] = mat_nt(weight_ref[...], low)[:, :group]
 
 
-def message_end(chunk, group, grad, back, other, normed, inv, gain, cls_rows, weight, passed):
+def message_end(chunk, group, grad, back, other, normed, inv, gain, cls_rows, weight):
     count, _, width = grad.shape
     rows = lambda columns: pl.BlockSpec((chunk, columns), lambda c: (c, 0))
     return call(
-        functools.partial(message_end_kernel, group, len(passed)),
+        functools.partial(message_end_kernel, group),
         "message_end",
+        0.0,
         grid=(count // chunk,),
-        in_specs=[pl.BlockSpec((chunk, 1, width), lambda c: (c, 0, 0))] + [rows(width)] * 3 + [rows(1), whole(gain), rows(width), whole(weight)]
-        + [ANY] * len(passed),
-        out_specs=[fixed((width, width)), fixed((8, width)), fixed((width, group))] + [ANY] * len(passed),
-        out_shape=[shaped((width, width), F32), shaped((8, width), F32), shaped((width, group), F32)]
-        + [shaped(v.shape, v.dtype) for v in passed],
-        input_output_aliases={8 + i: 3 + i for i in range(len(passed))},
-    )(grad, back, other, normed, inv, gain, cls_rows, weight, *passed)
+        in_specs=[pl.BlockSpec((chunk, 1, width), lambda c: (c, 0, 0))] + [rows(width)] * 3 + [rows(1), whole(gain), rows(width), whole(weight)],
+        out_specs=[fixed((width, width)), fixed((8, width)), fixed((width, group))],
+        out_shape=[shaped((width, width), F32), shaped((8, width), F32), shaped((width, group), F32)],
+    )(grad, back, other, normed, inv, gain, cls_rows, weight)
+
+
+def row_at(place_ref, base, moves):
+    at = base
+    for bit, rows, flipped in moves:
+        is_set = (place_ref[2] // bit) % 2
+        at = at + rows * ((1 - is_set) if flipped else is_set)
+    return pl.multiple_of(at, ROW_TILE)
+
+
+def add_kernel(sums, waits, outs, place_ref, *refs):
+    count = max(i for _, rows, _ in sums for i, _, _ in rows) + 1
+    terms, refs = refs[:count], refs[count + waits :]
+    out_refs, sem = refs[:outs], refs[-1]
+    bufs = refs[outs:-1]
+    copies = []
+    for n, (_, rows, size) in enumerate(sums):
+        for j, (i, base, moves) in enumerate(rows):
+            source = terms[i].at[pl.ds(row_at(place_ref, base, moves), size)]
+            copies.append(pltpu.make_async_copy(source, bufs[n].at[j], sem.at[len(copies)]))
+    for copy in copies:
+        copy.start()
+    done = 0
+    for n, ((out, at), rows, size) in enumerate(sums):
+        for copy in copies[done : done + len(rows)]:
+            copy.wait()
+        done += len(rows)
+        step = size // 2 if size % (2 * ROW_TILE) == 0 else size
+        for r in range(0, size, step):
+            total = bufs[n][0, r : r + step].astype(F32)
+            for j in range(1, len(rows)):
+                total += bufs[n][j, r : r + step].astype(F32)
+            out_refs[out][at + r : at + r + step] = total.astype(LOW)
+
+
+def added(place, sums, after=(), together=False):
+    arrays, listed = [], []
+    for terms, size in sums:
+        rows = []
+        for array, base, moves in terms:
+            known = [i for i, other in enumerate(arrays) if other is array]
+            if not known:
+                arrays.append(array)
+            rows.append((known[0] if known else len(arrays) - 1, base, moves))
+        to = (0, sum(other[2] for other in listed)) if together else (len(listed), 0)
+        listed.append((to, rows, size))
+    width = arrays[0].shape[1]
+    sizes = [sum(item[2] for item in listed)] if together else [item[2] for item in listed]
+    return call(
+        functools.partial(add_kernel, listed, len(after), len(sizes)),
+        "added",
+        in_specs=[SMEM] + [ANY] * (len(arrays) + len(after)),
+        out_specs=[VMEM] * len(sizes),
+        out_shape=[shaped((size, width), LOW) for size in sizes],
+        scratch_shapes=[pltpu.VMEM((len(rows), size, width), LOW) for _, rows, size in listed]
+        + [pltpu.SemaphoreType.DMA((sum(len(rows) for _, rows, _ in listed),))],
+    )(place, *arrays, *after)
+
+
+def join_kernel(bits, waits, place_ref, *refs):
+    count = len(bits)
+    pairs, refs = [refs[2 * i : 2 * i + 2] for i in range(count)], refs[2 * count + waits :]
+    *out_refs, buf, sem = refs
+    size = pairs[0][0].shape[0]
+    copies = []
+    for n, bit in enumerate(bits):
+        for i, ref in enumerate(pairs[n]):
+            at = row_at(place_ref, n * 2 * size, [(bit, size, i == 1)])
+            copies.append(pltpu.make_async_copy(ref, buf.at[pl.ds(at, size)], sem.at[n, i]))
+    for copy in copies:
+        copy.start()
+    for copy in copies:
+        copy.wait()
+    first = 0
+    for ref in out_refs:
+        rows = ref.shape[0]
+        step = rows // 2 if rows % (2 * ROW_TILE) == 0 else rows
+        for at in range(0, rows, step):
+            ref[at : at + step] = buf[first + at : first + at + step].astype(ref.dtype)
+        first += rows
+
+
+def joined(place, pairs, bits, dtype, after=(), splits=None):
+    size, width = pairs[0][0].shape
+    count = len(pairs)
+    outs = [(rows, width) for rows in splits or [2 * size] * count]
+    return call(
+        functools.partial(join_kernel, bits, len(after)),
+        "joined",
+        in_specs=[SMEM] + [ANY] * (2 * count + len(after)),
+        out_specs=[VMEM] * len(outs),
+        out_shape=[shaped(out, dtype) for out in outs],
+        scratch_shapes=[pltpu.VMEM((2 * size * count, width), LOW), pltpu.SemaphoreType.DMA((count, 2))],
+    )(place, *[ref for pair in pairs for ref in pair], *after)
 
 
 def gate_kernel(*refs):
@@ -687,7 +791,7 @@
 
 def gate(arrays, after, micros=0.0):
     count = len(arrays)
-    return call(
+    return list(call(
         gate_kernel,
         "gate",
         micros,
@@ -695,52 +799,32 @@
         out_specs=[ANY] * count,
         out_shape=[shaped(v.shape, v.dtype) for v in arrays],
         input_output_aliases={i: i for i in range(count)},
-    )(*arrays, *after)
-
-
-def merge_kernel(count, ordered, place_ref, *refs):
-    refs, out_ref = refs[:-1], refs[-1]
-    size = refs[0].shape[0] - count
-    total = refs[0][:count]
-    for ref in refs[1:]:
-        total += ref[:count]
-    out_ref[:count] = total
-    for k, ref in enumerate(refs):
-        at = (place_ref[0] ^ k) if ordered else k
-        out_ref[pl.ds(count + at * size, size)] = ref[count:]
-
-
-def merge(place, count, buffers, ordered=False):
-    rows, one, width = buffers[0].shape
-    return call(
-        functools.partial(merge_kernel, count, ordered),
-        "merge",
-        in_specs=[SMEM] + [VMEM] * len(buffers),
-        out_specs=VMEM,
-        out_shape=shaped((count + (rows - count) * len(buffers), one, width), F32),
-    )(place, *buffers)
+    )(*arrays, *after))
 
 
 def collect_kernel(place_ref, *refs):
-    *pieces, grad_cls_ref, out_ref = refs
-    frames, part, patches = pieces[0].shape
+    *pieces, grad_cls_ref, tok_ref, grad_ref = refs
+    frames, _, part, patches = pieces[0].shape
     own = grad_cls_ref[pl.ds(pl.multiple_of(place_ref[0] * part, part), part), :]
     lane = lax.broadcasted_iota(jnp.int32, (part, patches), 1)
     for j, piece in enumerate(reorder([ref[...] for ref in pieces], place_ref[0])):
         for f in range(frames):
             i = j * frames + f
-            out_ref[i] = jnp.where(lane == 0, piece[f].astype(F32) + own[:, i : i + 1], piece[f].astype(F32)).astype(LOW)
+            tok_ref[i] = piece[f, 0]
+            grad = piece[f, 1].astype(F32)
+            grad_ref[i] = jnp.where(lane == 0, grad + own[:, i : i + 1], grad).astype(LOW)
 
 
 def collect(place, pieces, grad_cls):
-    frames, part, patches = pieces[0].shape
+    frames, _, part, patches = pieces[0].shape
     shape = (frames * len(pieces), part, patches)
     return call(
         collect_kernel,
         "collect",
+        0.0,
         in_specs=[SMEM] + [VMEM] * (len(pieces) + 1),
-        out_specs=VMEM,
-        out_shape=shaped(shape, LOW),
+        out_specs=[VMEM] * 2,
+        out_shape=[shaped(shape, LOW)] * 2,
     )(place, *pieces, grad_cls)
 
 
@@ -753,8 +837,8 @@
     return one * 0.0
 
 
-def zero_of(array):
-    return nothing(array).astype(jnp.int32)
+def zero_of(*arrays):
+    return sum(nothing(array) for array in arrays).astype(jnp.int32)
 
 
 def frames_in(block, after):
@@ -781,35 +865,74 @@
     return [near, far, swap(near, "wide", 1), swap(far, "wide", 1)]
 
 
-def added(terms, start, size):
-    total = sum(
-        lax.dynamic_slice_in_dim(array, begin + start, size, 0).astype(F32) for array, begin in terms
-    )
-    return total.astype(LOW)
-
-
-def halve(terms, size, bit):
-    size = size // 2
-    odd = ((lax.axis_index("narrow") & bit) != 0).astype(jnp.int32)
-    sent = added(terms, (1 - odd) * size, size)
-    received = swap(sent, "narrow", bit)
-    return [(array, start + odd * size) for array, start in terms] + [(received, 0)], size, sent, received
-
-
-def halve_all(terms, size, bits):
-    for bit in bits:
-        terms, size, _, _ = halve(terms, size, bit)
-    return terms, size
-
-
-def join_all(block, bits):
-    for bit in reversed(bits):
-        odd = (lax.axis_index("narrow") & bit) != 0
-        other = swap(block, "narrow", bit)
-        block = jnp.where(
-            odd, jnp.concatenate([other, block], axis=0), jnp.concatenate([block, other], axis=0)
+def orders(count):
+    bits = bits_of(lax.axis_size("narrow"))[:count]
+    return [bits, bits[1:] + bits[:1]]
+
+
+def regions_of(arrays, base=0):
+    half = arrays[0].shape[0] // 2
+    return [[(array, n * half, []) for array in arrays] for n in range(2)], half
+
+
+def halving(place, regions, size, steps):
+    after = ()
+    for at in range(steps):
+        bits = [order[at] for order in orders(steps)]
+        size = size // 2
+        sums = [
+            ([(array, base, moves + [(bit, size, True)]) for array, base, moves in terms], size)
+            for bit, terms in zip(bits, regions)
+        ]
+        sent = added(place, sums, after)
+        received, after = yield sent, [swap(block, "narrow", bit) for block, bit in zip(sent, bits)]
+        regions = [
+            [(array, base, moves + [(bit, size, False)]) for array, base, moves in terms] + [(block, 0, [])]
+            for bit, terms, block in zip(bits, regions, received)
+        ]
+    return regions, size, after
+
+
+def joining(place, blocks, steps, splits):
+    for at in reversed(range(steps)):
+        bits = [order[at] for order in orders(steps)]
+        others, after = yield blocks, [swap(block, "narrow", bit) for block, bit in zip(blocks, bits)]
+        last = at == 0
+        blocks = joined(
+            place, list(zip(blocks, others)), bits, F32 if last else LOW, after, splits if last else None
         )
-    return block
+    return blocks
+
+
+def whole_sum(place, blocks, steps):
+    for bit in bits_of(lax.axis_size("narrow"))[steps:]:
+        others, after = yield blocks, [swap(block, "narrow", bit) for block in blocks]
+        blocks = added(
+            place, [([(a, 0, []), (b, 0, [])], a.shape[0]) for a, b in zip(blocks, others)], after
+        )
+    return blocks
+
+
+class Chain:
+    def __init__(self, steps):
+        self.steps = steps
+        self.value = None
+        self.turns = 0
+        self.sent, self.received = next(steps)
+
+    def turn(self, *after):
+        if self.value is not None:
+            return after[0]
+        self.turns += 1
+        try:
+            self.sent, self.received = self.steps.send((self.received, after))
+        except StopIteration as end:
+            self.value = end.value
+            return after[0] if isinstance(self.value, tuple) else self.value[0]
+        return self.sent[0]
+
+
+ORDER = "foAfoaPMBafaEfaCf"
 
 
 def body(
@@ -863,19 +986,26 @@
     cls_rows = jnp.concatenate(
         reorder([p[2:].reshape(group, part).astype(LOW) for p in packs], wide_idx), axis=1
     )
-    for bit in bits_of(narrow):
-        cls_rows = jnp.concatenate([cls_rows, swap(cls_rows, "narrow", bit)], axis=0)
-    toks = frames_in(tokens_t, packs[-1])
+    cls_own = cls_rows
+    toks = frames_in(tokens_t, cls_own)
     attn_own = jnp.concatenate(
         [qkv_weight.transpose(1, 2, 0).reshape(3 * part, width), out_weight], axis=0
     )
+    attn_near = send_half(attn_own, cls_own)
+    narrow_bits = bits_of(narrow)
+    cls_next = swap(cls_rows, "narrow", 1)
+    cls_rows = jnp.concatenate([cls_rows, cls_next], axis=0)
+    attn_near = gate(attn_near, [cls_next, toks[1]])
+    attn_far = [swap(near, "narrow", 1) for near in attn_near]
+    (cls_rows,) = gate([cls_rows], attn_near)
+    for bit in narrow_bits[1:]:
+        if bit == narrow_bits[-1]:
+            (cls_rows,) = gate([cls_rows], attn_far)
+        cls_rows = jnp.concatenate([cls_rows, swap(cls_rows, "narrow", bit)], axis=0)
     attn_weights = near_shards(attn_own)
-    attn_near = send_half(attn_own, packs[-1])
-    attn_far = [swap(near, "narrow", 1) for near in attn_near]
     for near, far in zip(attn_near, attn_far):
         attn_weights += far_shards(near, far)
-
-    cots = frames_in(cotangent.transpose(0, 2, 1), attn_far[0])
+    cots = frames_in(cotangent.transpose(0, 2, 1), attn_near[0])
 
     caption_slot = jnp.arange(caption_len.shape[1])
     word_total = jnp.sum(
@@ -890,11 +1020,11 @@
     msg_normed, msg_inv, msg_in, cross_heads, cross_prob, cross_mix, base, group_sum = message_forward(
         chunk, group, place, cls_rows, message_weight,
         (message_bias, message_gain, message_shift, cross_offset), cross_flat, cross_bias, cross_proj,
-        attn_far + toks[1:] + cots[1:],
+        attn_far + toks[1:],
     )
     group_sums = [group_sum] + [swap(group_sum, "wide", k) for k in range(1, wide)]
 
-    odd, begin = narrow_idx & 1, zero_of(group_sums[-1])
+    odd, begin = narrow_idx & 1, zero_of(*cots[2:])
     half = width // 2
     mlp_half = jnp.concatenate(
         [lax.dynamic_slice_in_dim(w, odd * half + begin, half, 0) for w in (up_weight, down_weight)], axis=0
@@ -904,7 +1034,7 @@
 
     (normed, inv, attn_in, heads, prob, mix, hidden_res, mlp_normed, mlp_inv, mlp_in) = attn_forward(
         seq_pad, place, (attn_gain, attn_shift, mlp_gain, mlp_shift), base, toks, group_sums, packs, attn_weights,
-        [up_shards[1], down_shards[1]],
+        [up_shards[1], down_shards[1]] + cots[1:],
     )
     mlp_in = mlp_in.reshape(rows, width)
     bits = bits_of(narrow)
@@ -914,16 +1044,40 @@
         frames, place, scale, mlp_in, packs[:2], up_shards + down_shards, cots=cots, after=mlp_near
     )
     *mlp_far, grad_next = gate([swap(near, "narrow", 1) for near in mlp_near] + [grad_own[1]], [acc])
-    own_terms = [(grad_own[0], 0), (swap(grad_next, "wide", 1), 0)]
-    own_terms, own_size, own_sent, own_received = halve(own_terms, size, bits[0])
+    def split_steps(rows):
+        count = 0
+        while count < len(bits) and rows % (2 * ROW_TILE) == 0:
+            rows, count = rows // 2, count + 1
+        return count
+
+    mlp_steps, attn_count = split_steps(size // 2), split_steps(2 * part)
+    own = Chain(halving(place, *regions_of([grad_own[0], swap(grad_next, "wide", 1)]), mlp_steps))
     mlp_weights = [piece for near, far in zip(mlp_near, mlp_far) for piece in far_shards(near, far)]
     acc, gacc, sum_up_far, *grad_far = mlp_step(
-        frames, place, scale, mlp_in, packs[2:], mlp_weights, carried=(grad_rows, acc, gacc), after=[own_sent]
+        frames, place, scale, mlp_in, packs[2:], mlp_weights, carried=(grad_rows, acc, gacc), after=own.sent
     )
-    grad_far = gate(grad_far, [own_received])
-    own_terms, own_size, own_sent, own_next = halve(own_terms, own_size, bits[1])
-    far_terms = [(grad_far[0], 0), (swap(grad_far[1], "wide", 1), 0)]
-    far_terms, far_size, far_sent, far_received = halve(far_terms, size, bits[0])
+
+    def far_steps(arrays):
+        regions, left, after = yield from halving(place, *regions_of(arrays), mlp_steps)
+        value = added(place, [(terms, left) for terms in regions], after, True)
+        crossed, after = yield value, [swap(value[0], "wide", 2)]
+        blocks = added(
+            place,
+            [(terms + [(crossed[0], n * left, [])], left) for n, terms in enumerate(own.value[0])],
+            after,
+        )
+        blocks = yield from whole_sum(place, blocks, mlp_steps)
+        return (yield from joining(place, blocks, mlp_steps, [width, hidden]))
+
+    def attn_steps(arrays):
+        regions, left, after = yield from halving(place, *regions_of(arrays), attn_count)
+        blocks = added(place, [(terms, left) for terms in regions], after)
+        blocks = yield from whole_sum(place, blocks, attn_count)
+        return (yield from joining(place, blocks, attn_count, [3 * part, part]))
+
+    own.turn(acc)
+    grad_far = gate(grad_far, own.sent)
+    far = Chain(far_steps([grad_far[0], swap(grad_far[1], "wide", 1)]))
 
     shape = (frames, seq_pad, width)
     per_frame = (
@@ -931,53 +1085,61 @@
     )
     *blocks, proj, low, sums = attn_backward(
         patches, place, scale, (attn_gain, mlp_gain), per_frame, packs, [sum_up, sum_up_far], attn_weights,
-        [own_sent, far_sent],
+        own.sent + far.sent,
     )
-    grad_attn = list(attn_grads(attn_in, proj, low, mix, 1, [far_received, own_next]))
-    half = 2 * part
-    attn_far = [(grad_attn[0], 0), (swap(grad_attn[1], "wide", 1), 0)]
-    attn_sent = added(attn_far, 0, 2 * half)
-    attn_received = swap(attn_sent, "wide", 2)
-    grad_attn = gate(attn_grads(attn_in, proj, low, mix, 0, [attn_sent]), [attn_received])
-    attn_own = [(grad_attn[0], 0), (swap(grad_attn[1], "wide", 1), 0)]
-
-    own_terms, own_size = halve_all(own_terms, own_size, bits[2:])
-    far_terms, far_size = halve_all(far_terms, far_size, bits[1:])
-    crossed = swap(added(far_terms, 0, far_size), "wide", 2)
-    grad_mlp = join_all(added(own_terms + [(crossed, 0)], 0, own_size), bits).astype(F32)
-    grad_attn_own = []
-    for at in (0, half):
-        terms, left = halve_all([(array, at) for array, _ in attn_own + [(attn_received, 0)]], half, bits)
-        grad_attn_own.append(join_all(added(terms, 0, left), bits))
-    grad_attn_own = jnp.concatenate(grad_attn_own, axis=0).astype(F32)
-
-    (sums,) = gate([sums], [far_received, own_next])
     count = 8 + wide
-    sums = merge(place, count, [sums] + [swap(sums, "wide", k) for k in range(1, wide)], True)
-    for bit in bits:
-        sums = merge(place, count, [sums, swap(sums, "narrow", bit)])
-    grad_msg = sums[count:]
-    sums = sums[:count].reshape(count, width)
+    gathered = lax.all_gather(sums, ("narrow", "wide"))
+    far.turn(own.turn(low))
+    grad_attn = attn_grads(attn_in, proj, low, mix, own.sent + far.sent)
+    last = grad_attn[0]
+    while far.turns < mlp_steps - 1:
+        last = far.turn(last)
+    grad_attn = gate(grad_attn, [last])
+    attn_next, attn_last = (swap(grad_attn[k], "wide", 1) for k in (1, 3))
+    last = added(place, [([(grad_attn[2], 0, []), (attn_last, 0, [])], 4 * part)])[0]
+    attn_received = swap(last, "wide", 2)
+    attn = pieces = None
+    for step in ORDER:
+        if step == "f":
+            while far.turns == mlp_steps and own.value is None:
+                last = own.turn(last)
+            last = far.turn(last)
+        elif step == "o":
+            last = own.turn(last)
+        elif step == "a":
+            last = attn.turn(last)
+        elif step == "A":
+            attn_received, attn_next = gate([attn_received, attn_next], [last, *own.received])
+            attn = Chain(attn_steps([grad_attn[0], attn_next, attn_received]))
+            last = attn.sent[0]
+        elif step == "P":
+            blocks = gate(blocks, [last])
+            pieces = [piece if k == 0 else swap(piece, "wide", k) for k, piece in enumerate(blocks)]
+        elif step == "M":
+            grad_msg, sums, grad_cross_flat, grad_cross_proj, sum_cross_grad, sum_cross, back = message_backward(
+                place, count, wide, gathered, msg_in, cross_heads, cross_prob, cross_mix, cross_flat, cross_proj, [last]
+            )
+            last = back
+        elif step == "B":
+            for bit in bits_of(wide)[:-1]:
+                back = back + gate([swap(back, "wide", bit)], [last])[0]
+            other = swap(back.astype(LOW), "wide", bits_of(wide)[-1])
+            last = back
+        elif step == "E":
+            grad_message_weight, msg_sums, grad_cls = message_end(
+                chunk, group, grad_msg, back, gate([other], [last])[0], msg_normed, msg_inv, message_gain, cls_rows,
+                message_weight,
+            )
+            last = grad_message_weight
+        elif step == "C":
+            output_tokens, grad_tokens = collect(place, pieces[:1] + gate(pieces[1:], [last]), grad_cls)
+            last = grad_tokens
+    while attn.value is None or far.value is None:
+        while far.turns == mlp_steps and own.value is None:
+            last = own.turn(last)
+        last = far.turn(attn.turn(last))
+    sums = sums.reshape(count, width)
     grad_up_bias = lax.dynamic_slice_in_dim(sums[6 : 6 + wide].reshape(-1), wide_idx * hidden, hidden, 0)
-
-    grad_cross_flat, grad_cross_proj, sum_cross_grad, sum_cross, back = message_backward(
-        grad_msg, msg_in, cross_heads, cross_prob, cross_mix, cross_flat, cross_proj, [attn_received]
-    )
-    bits = bits_of(wide)
-    for bit in bits[:-1]:
-        back = back + swap(back, "wide", bit)
-    grad_message_weight, msg_sums, grad_cls, *blocks = message_end(
-        chunk, group, grad_msg, back, swap(back.astype(LOW), "wide", bits[-1]), msg_normed, msg_inv, message_gain, cls_rows,
-        message_weight, blocks,
-    )
-
-    def frames_out(pieces):
-        return [piece if k == 0 else swap(piece, "wide", k) for k, piece in enumerate(pieces)]
-
-    out_pieces = frames_out(blocks[:wide])
-    grad_pieces = frames_out(blocks[wide:])
-    output_tokens = jnp.concatenate(reorder(out_pieces, wide_idx), axis=0)
-    grad_tokens = collect(place, grad_pieces, grad_cls)
 
     return (
         output_tokens.transpose(0, 2, 1),
@@ -992,15 +1154,15 @@
         sum_cross_grad[0],
         sums[4],
         sums[5],
-        grad_attn_own[: 3 * part].reshape(3, part, width).transpose(2, 0, 1),
+        attn.value[0].reshape(3, part, width).transpose(2, 0, 1),
         own_cols(sums[count - 2 :]),
-        grad_attn_own[3 * part :],
+        attn.value[1],
         own_cols(sums[3]),
         sums[1],
         sums[2],
-        grad_mlp[:width],
+        far.value[0],
         grad_up_bias,
-        grad_mlp[width:],
+        far.value[1],
         own_cols(sums[0]),
     )
 

time: 446 us -> 417 us (0.935)
  waiting for transfers between devices: 187 us -> 112 us
  Pallas kernels: 119 us -> 169 us
  other arithmetic: 37.3 us -> 10.2 us
  between operations: 4.32 us -> 19 us
  starting transfers between devices: 56.3 us -> 64.9 us
    ppermute x67, waiting for transfers between devices: 187 us -> 112 us  [swap(): lax.ppermute(block, axis, [(i, i ^ flip) for i in range(lax.axis_size(axi...]
    pallas_call x9 -> x23, Pallas kernels: 29 us -> 79.1 us  [the longest x13 39.3 us: added(): call(functools.partial(add_kernel, listed, len(after), len(sizes)), 'adde...]
    convert_element_type x17 -> x1, other arithmetic: 24.4 us -> 1.8 us  [body(): other = swap(back.astype(LOW), 'wide', bits_of(wide)[-1])]
    unnamed x146 -> x200, local copies, waits for them, and re-layouts: 16.2 us -> 25.6 us
    ppermute x67, starting transfers between devices: 56.3 us -> 64.8 us  [swap(): lax.ppermute(block, axis, [(i, i ^ flip) for i in range(lax.axis_size(axi...]
    slice x3 -> x0, local copies, waits for them, and re-layouts: 5.55 us -> none  [the longest x1 2.49 us: body(): grad_mlp[width:]]
  transfers between devices with their start and end apart: 67 -> 68, of which waited for: 34 -> 29; matrix products, arithmetic and copies ran while one was open for 11% -> 5% of each run, Pallas kernels for 26% -> 37%
where the time goes in v1:
time: 417 us; the launch traced here: 412 us
  Pallas kernels  169 us (41%)
  waiting for transfers between devices  112 us (27%)
  starting transfers between devices  64.9 us (16%)
  local copies, waits for them, and re-layouts  36.7 us (9%)
  between operations  19 us (5%)
  other arithmetic  10.2 us (2%)
    ppermute x67, waiting for transfers between devices, swap(): lax.ppermute(block, axis, [(i, i ^ flip) for i in range(lax.axis_size(axi...  112 us
    ppermute x67, starting transfers between devices, swap(): lax.ppermute(block, axis, [(i, i ^ flip) for i in range(lax.axis_size(axi...  64.8 us
    pallas_call x13, Pallas kernels, added(): call(functools.partial(add_kernel, listed, len(after), len(sizes)), 'adde...  39.3 us
    pallas_call x2, Pallas kernels, mlp_step(): call(functools.partial(mlp_kernel, frames, count, first, len(after)), 'ml...  39.2 us
    unnamed x200, local copies, waits for them, and re-layouts  25.6 us
    pallas_call x1, Pallas kernels, attn_backward(): call(functools.partial(attn_backward_kernel, shards, len(after)), 'attn_b...  24.1 us
    pallas_call x1, Pallas kernels, attn_forward(): call(functools.partial(attn_forward_kernel, len(after)), 'attn_forward',...  22.6 us
    pallas_call x6, Pallas kernels, joined(): call(functools.partial(join_kernel, bits, len(after)), 'joined', in_specs...  19 us
  transfers between devices with their start and end apart: 68, of which 29 were waited for; matrix products, arithmetic and copies ran while one was open for 5% of the time, Pallas kernels for 37%

profile of v1, /device:TPU:0, one launch (start us, length us, event | category | flops | bytes accessed | tf_op | source)
XLA Modules:
  0.0 411.7 jit_solution(4731977295438838185)
XLA Ops:
  8.9 2.4 collective-permute-start
  12.9 2.2 collective-permute-done.1.refs_10_.refs_0_.refs_2_
  25.4 8.9 %collective-permute-done.4.refs_0_ = bf16[384,768]{1,0:T(8,128)(2,1)S(1)} collective-permute-done((bf16[384,768]{1,0:T(8,128)(2,1)S(1)}, bf16[384,768]{1,0:T(8,128)(2,1)S(1)}, u32[]{:S(2)}, u32[]{:S(2)}) %collective-permute-start.4) | collective-permute-done | bytes 589856 | tf_op jit(solution)/shard_map/ppermute | solution.py:832
  41.0 1.6 collective-permute-start.6
  42.7 2.5 collective-permute-done.6
  47.9 6.8 %collective-permute-done.21.refs_22_.refs_5_ = bf16[3,192,197]{2,1,0:T(8,128)(2,1)S(1)} collective-permute-done((bf16[3,192,197]{2,1,0:T(8,128)(2,1)}, bf16[3,192,197]{2,1,0:T(8,128)(2,1)S(1)}, u32[]{:S(2)}, u32[]{:S(2)}) %collective-permute-start.21) | collective-permute-done | bytes 226976 | tf_op jit(solution)/shard_map/ppermute | solution.py:832
  61.2 2.7 collective-permute-done.9.refs_2_
  63.8 2.6 collective-permute-start.8
  66.7 2.7 collective-permute-done.8
  70.1 4.0 message_forward.1
  81.2 22.6 %attn_forward.1 = (f32[3,208,768]{2,1,0:T(8,128)}, f32[3,208,1]{2,1,0:T(8,128)}, bf16[3,208,768]{2,1,0:T(8,128)(2,1)}, bf16[3,4,3,208,192]{4,3,2,1,0:T(8,128)(2,...) custom-call(s32[3]{0:T(128)} %pad_add_fusion.place_ref, ...), custom_call_target="tpu_custom_call" | custom-call | flops 23000000512 | bytes 69000000 | tf_op jit(solution)/shard_map/attn_forward/pallas_call | solution.py:233
  103.7 1.8 collective-permute-done.22.refs_0_
  107.7 19.2 %mlp.2 = (bf16[3,208,768]{2,1,0:T(8,128)(2,1)}, bf16[624,768]{1,0:T(8,128)(2,1)}, f32[624,768]{1,0:T(8,128)}, f32[624,768]{1,0:T(8,128)}, f32[2,1,768]{2,1,0:T(1...) custom-call(s32[3]{0:T(128)} %pad_add_fusion.place_ref, f32[3]{0:T(128)} %select_reduce_fusion.1.scale_ref, ...), custom_call_target="tpu_custom_call" | custom-call | flops 19499999232 | bytes 58500000 | tf_op jit(solution)/shard_map/mlp/pallas_call | solution.py:358
  126.9 7.9 %collective-permute-done.23.refs_0_ = bf16[768,768]{1,0:T(8,128)(2,1)S(1)} collective-permute-done((bf16[768,768]{1,0:T(8,128)(2,1)}, bf16[768,768]{1,0:T(8,128)(2,1)S(1)}, u32[]{:S(2)}, u32[]{:S(2)}) %collective-permute-start.23) | collective-permute-done | bytes 1179680 | tf_op jit(solution)/shard_map/ppermute | solution.py:832
  137.6 3.0 collective-permute-done.26.refs_1_
  141.9 3.3 added.13
  146.1 1.6 collective-permute-start.28
  149.1 20.0 %mlp.3 = (f32[624,768]{1,0:T(8,128)}, f32[624,768]{1,0:T(8,128)}, f32[2,1,768]{2,1,0:T(1,128)}, bf16[1536,768]{1,0:T(8,128)(2,1)}, bf16[1536,768]{1,0:T(8,128)(2,1)}) custom-call(s32[3]{0:T(128)} %pad_add_fusion.place_ref, f32[3]{0:T(128)} %select_reduce_fusion.1.scale_ref, bf16[624,768]{1,0:T(8,128)(2,1)} %bitcast.70, f32[5,768]{1,0:T(8,128)} %copy-done.81, ...), custom_call_target="tpu_custom_call" | custom-call | flops 19499999232 | bytes 58500000 | tf_op jit(solution)/shard_map/mlp/pallas_call | solution.py:358
  170.1 3.0 added.14
  174.6 2.9 collective-permute-start.31
  179.4 3.3 added.15
  185.4 24.1 %attn_backward.1 = (bf16[3,2,192,197]{3,2,1,0:T(8,128)(2,1)}, bf16[3,2,192,197]{3,2,1,0:T(8,128)(2,1)}, bf16[3,2,192,197]{3,2,1,0:T(8,128)(2,1)}, bf16[3,2,192,1...) custom-call(s32[3]{0:T(128)} %pad_add_fusion.place_ref, ...), custom_call_target="tpu_custom_call" | custom-call | flops 24000000000 | bytes 72000000 | tf_op jit(solution)/shard_map/attn_backward/pallas_call | solution.py:460
  210.2 2.8 added.16
  214.1 3.0 added.17
  217.8 3.3 collective-permute-start.35
  221.1 8.1 %attn_grads.1 = (bf16[768,768]{1,0:T(8,128)(2,1)}, bf16[768,768]{1,0:T(8,128)(2,1)}, bf16[768,768]{1,0:T(8,128)(2,1)}, bf16[768,768]{1,0:T(8,128)(2,1)}) custom-call(bf16[624,768]{1,0:T(8,128)(2,1)} %bitcast.67, bf16[624,768]{1,0:T(8,128)(2,1)} %bitcast.62, bf16[3,4,208,576]{3,2,1,0:T(8,128)(2,1)} %get-tuple-element.164.proj_ref, ...), custom_call_target="tpu_custom_call" | custom-call | tf_op jit(solution)/shard_map/attn_grads/pallas_call | solution.py:503
  229.2 2.1 collective-permute-done.34.refs_3_
  231.3 3.2 collective-permute-done.35.refs_5_.refs_6_
  235.2 2.8 added.18
  238.7 2.5 collective-permute-done.36.refs_1_
  242.2 3.7 added.19.refs_8_
  248.3 2.9 collective-permute-start.41
  251.1 9.8 %collective-permute-done.39.refs_4_ = bf16[96,768]{1,0:T(8,128)(2,1)S(1)} collective-permute-done((bf16[96,768]{1,0:T(8,128)(2,1)S(1)}, bf16[96,768]{1,0:T(8,128)(2,1)S(1)}, u32[]{:S(2)}, u32[]{:S(2)}) %collective-permute-start.39) | collective-permute-done | bytes 147488 | tf_op jit(solution)/shard_map/ppermute | solution.py:832
  263.1 3.0 added.20.refs_2_
  267.3 10.4 %collective-permute-done.37.refs_0_ = bf16[768,768]{1,0:T(8,128)(2,1)S(1)} collective-permute-done((bf16[768,768]{1,0:T(8,128)(2,1)}, bf16[768,768]{1,0:T(8,128)(2,1)S(1)}, u32[]{:S(2)}, u32[]{:S(2)}) %collective-permute-start.37) | collective-permute-done | bytes 1179680 | tf_op jit(solution)/shard_map/ppermute | solution.py:832
  278.7 3.0 added.21
  284.5 3.1 added.22
  287.6 2.0 collective-permute-done.43.refs_3_
  291.7 2.8 added.23
  294.6 5.1 %message_backward.1 = (f32[96,1,768]{2,1,0:T(1,128)}, f32[12,1,768]{2,1,0:T(1,128)}, f32[576,768]{1,0:T(8,128)}, f32[192,768]{1,0:T(8,128)}, f32[1,768]{1,0:T(1,...) custom-call(s32[3]{0:T(128)} %pad_add_fusion.place_ref, f32[32,15,1,768]{3,2,1,0:T(1,128)} %bitcast.66, ...), custom_call_target="tpu_custom_call" | custom-call | tf_op jit(solution)/shard_map/message_backward/pallas_call | solution.py:645
  299.7 2.4 collective-permute-start.54
  302.5 1.7 collective-permute-start.49
  305.6 1.8 fusion.1
  307.4 3.7 collective-permute-done.49.refs_4_
  311.2 5.2 %collective-permute-done.50.refs_6_.refs_7_ = bf16[96,768]{1,0:T(8,128)(2,1)S(1)} collective-permute-done((bf16[96,768]{1,0:T(8,128)(2,1)S(1)}, bf16[96,768]{1,0:T(8,128)(2,1)S(1)}, u32[]{:S(2)}, u32[]{:S(2)}) %collective-permute-start.50) | collective-permute-done | bytes 147488 | tf_op jit(solution)/shard_map/ppermute | solution.py:832
  317.1 2.7 added.24
  320.5 2.7 joined.6
  323.6 3.4 collective-permute-start.59
  328.0 15.7 %collective-permute-done.52.refs_5_ = bf16[48,768]{1,0:T(8,128)(2,1)S(1)} collective-permute-done((bf16[48,768]{1,0:T(8,128)(2,1)}, bf16[48,768]{1,0:T(8,128)(2,1)S(1)}, u32[]{:S(2)}, u32[]{:S(2)}) %collective-permute-start.52) | collective-permute-done | bytes 73760 | tf_op jit(solution)/shard_map/ppermute | solution.py:832
  344.3 2.8 added.25
  349.6 4.0 message_end.1
  353.6 3.1 joined.7
  356.8 1.7 collective-permute-start.65
  359.1 2.9 collective-permute-start.66
  363.9 2.4 joined.8
  366.5 1.9 collective-permute-start.62
  368.4 3.4 collective-permute-done.48.refs_2_
  372.6 3.6 collect.1
  376.2 5.3 %collective-permute-done.61.refs_1_ = bf16[96,768]{1,0:T(8,128)(2,1)S(1)} collective-permute-done((bf16[96,768]{1,0:T(8,128)(2,1)}, bf16[96,768]{1,0:T(8,128)(2,1)S(1)}, u32[]{:S(2)}, u32[]{:S(2)}) %collective-permute-start.61) | collective-permute-done | bytes 147488 | tf_op jit(solution)/shard_map/ppermute | solution.py:832
  382.2 2.7 joined.9
  385.8 1.6 collective-permute-start.64
  390.1 2.9 collective-permute-done.63.refs_1_
  394.6 3.4 joined.10
  399.7 4.6 %joined.11 = (f32[768,768]{1,0:T(8,128)}, f32[768,768]{1,0:T(8,128)}) custom-call(s32[3]{0:T(128)} %pad_add_fusion.place_ref, bf16[384,768]{1,0:T(8,128)(2,1)} %get-tuple-element.208.refs_4_.refs_0_, bf16[384,768]{1,0:T(8,128)(2,1)} %copy-done.38, bf16[384,768]{1,0:T(8,128)(2,1)} %get-tuple-element.227.refs_2_, bf16[384,768]{1,0:T(8,128)(2,1)} %copy-done.39, ...), custom_call_target="tpu_custom_call" | custom-call | tf_op jit(solution)/shard_map/joined/pallas_call | solution.py:778
  (357 shorter events, 84.4 us)
Async XLA Ops:
  7.3 287.3 %all-gather.3.cloned.1.call-start = ((), (), s32[]{:S(2)}) async-start(), calls=%async_computation | async-start | bytes 1520640 | tf_op jit(solution)/shard_map/all_gather | solution.py:1091
  8.9 4.0 collective-permute-start
  18.0 16.3 %collective-permute-start.4 = (bf16[384,768]{1,0:T(8,128)(2,1)S(1)}, bf16[384,768]{1,0:T(8,128)(2,1)S(1)}, u32[]{:S(2)}, u32[]{:S(2)}) collective-permute-start(bf16[384,768]{1,0:T(8,128)(2,1)S(1)} %fusion), channel_id=1, source_target_pairs={{0,2},{1,3},{2,0},{3,1},{4,6},{5,7},{6,4},{7,5},{8,10},{9,11},{10,... | collective-permute-start | bytes 1769480 | tf_op jit(solution)/shard_map/ppermute | solution.py:832
  19.9 54.2 %collective-permute-start.14 = (bf16[768,768]{1,0:T(8,128)(2,1)}, bf16[768,768]{1,0:T(8,128)(2,1)}, u32[]{:S(2)}, u32[]{:S(2)}) collective-permute-start(bf16[768,768]{1,0:T(8,128)(2,1)} %pad_maximum_fusion.refs_12_.refs_6_), channel_id=1, source_target_pairs={{0,1},{1,0},{2,3},{3,2},{4,5},{5,4},{6,7},{7,6},{8,9},{9,8},{10,11... | collective-permute-start | bytes 3538952 | tf_op jit(solution)/shard_map/ppermute | solution.py:832
  20.9 4.5 %collective-permute-start.5 = (bf16[3,192,197]{2,1,0:T(8,128)(2,1)S(1)}, bf16[3,192,197]{2,1,0:T(8,128)(2,1)S(1)}, u32[]{:S(2)}, u32[]{:S(2)}) collective-permute-start(bf16[3,192,197]{2,1,0:T(8,128)(2,1)S(1)} %get-tuple-element.245), channel_id=1, source_target_pairs={{0,1},{1,0},{2,3},{3,2},{4,5},{5,4},{6,7},{7,6},{8,9},{9,8},{10,11... | collective-permute-start | bytes 680840 | tf_op jit(solution)/shard_map/ppermute | solution.py:832
  21.6 3.8 collective-permute-start.3
  24.3 18.3 %collective-permute-start.10 = (bf16[3,192,197]{2,1,0:T(8,128)(2,1)}, bf16[3,192,197]{2,1,0:T(8,128)(2,1)}, u32[]{:S(2)}, u32[]{:S(2)}) collective-permute-start(bf16[3,192,197]{2,1,0:T(8,128)(2,1)} %get-tuple-element.246), channel_id=1, source_target_pairs={{0,3},{1,2},{2,1},{3,0},{4,7},{5,6},{6,5},{7,4},{8,11},{9,10},{10,... | collective-permute-start | bytes 680840 | tf_op jit(solution)/shard_map/ppermute | solution.py:832
  38.1 7.4 %collective-permute-start.20 = (bf16[3,192,197]{2,1,0:T(8,128)(2,1)}, bf16[3,192,197]{2,1,0:T(8,128)(2,1)S(1)}, u32[]{:S(2)}, u32[]{:S(2)}) collective-permute-start(bf16[3,192,197]{2,1,0:T(8,128)(2,1)} %get-tuple-element.240), channel_id=1, source_target_pairs={{0,2},{1,3},{2,0},{3,1},{4,6},{5,7},{6,4},{7,5},{8,10},{9,11},{10,... | collective-permute-start | bytes 680840 | tf_op jit(solution)/shard_map/ppermute | solution.py:832
  39.5 20.2 %collective-permute-start.7 = (bf16[384,768]{1,0:T(8,128)(2,1)S(1)}, bf16[384,768]{1,0:T(8,128)(2,1)S(1)}, u32[]{:S(2)}, u32[]{:S(2)}) collective-permute-start(bf16[384,768]{1,0:T(8,128)(2,1)S(1)} %copy-done.13), channel_id=1, source_target_pairs={{0,4},{4,0},{8,12},{12,8},{16,20},{20,16},{24,28},{28,24},{1,5},{5... | collective-permute-start | bytes 1769480 | tf_op jit(solution)/shard_map/ppermute | solution.py:832
  41.0 4.2 %collective-permute-start.6 = (bf16[24,768]{1,0:T(8,128)(2,1)}, bf16[24,768]{1,0:T(8,128)(2,1)S(1)}, u32[]{:S(2)}, u32[]{:S(2)}) collective-permute-start(bf16[24,768]{1,0:T(8,128)(2,1)} %gate.13), channel_id=1, source_target_pairs={{0,8},{4,12},{8,0},{12,4},{16,24},{20,28},{24,16},{28,20},{1,9},{5... | collective-permute-start | bytes 110600 | tf_op jit(solution)/shard_map/ppermute | solution.py:832
  42.6 32.1 %collective-permute-start.17 = (bf16[768,768]{1,0:T(8,128)(2,1)S(1)}, bf16[768,768]{1,0:T(8,128)(2,1)}, u32[]{:S(2)}, u32[]{:S(2)}) collective-permute-start(bf16[768,768]{1,0:T(8,128)(2,1)S(1)} %copy-done.43), channel_id=1, source_target_pairs={{0,1},{1,0},{2,3},{3,2},{4,5},{5,4},{6,7},{7,6},{8,9},{9,8},{10,11... | collective-permute-start | bytes 3538952 | tf_op jit(solution)/shard_map/ppermute | solution.py:832
  45.2 30.9 %collective-permute-start.18 = (bf16[768,768]{1,0:T(8,128)(2,1)}, bf16[768,768]{1,0:T(8,128)(2,1)}, u32[]{:S(2)}, u32[]{:S(2)}) collective-permute-start(bf16[768,768]{1,0:T(8,128)(2,1)} %refs_8_.1), channel_id=1, source_target_pairs={{0,1},{1,0},{2,3},{3,2},{4,5},{5,4},{6,7},{7,6},{8,9},{9,8},{10,11... | collective-permute-start | bytes 3538952 | tf_op jit(solution)/shard_map/ppermute | solution.py:832
  45.5 9.2 %collective-permute-start.21 = (bf16[3,192,197]{2,1,0:T(8,128)(2,1)}, bf16[3,192,197]{2,1,0:T(8,128)(2,1)S(1)}, u32[]{:S(2)}, u32[]{:S(2)}) collective-permute-start(bf16[3,192,197]{2,1,0:T(8,128)(2,1)} %get-tuple-element.242), channel_id=1, source_target_pairs={{0,3},{1,2},{2,1},{3,0},{4,7},{5,6},{6,5},{7,4},{8,11},{9,10},{10,... | collective-permute-start | bytes 680840 | tf_op jit(solution)/shard_map/ppermute | solution.py:832
  54.7 9.2 %collective-permute-start.9 = (bf16[3,192,197]{2,1,0:T(8,128)(2,1)S(1)}, bf16[3,192,197]{2,1,0:T(8,128)(2,1)}, u32[]{:S(2)}, u32[]{:S(2)}) collective-permute-start(bf16[3,192,197]{2,1,0:T(8,128)(2,1)S(1)} %copy-done.45), channel_id=1, source_target_pairs={{0,2},{1,3},{2,0},{3,1},{4,6},{5,7},{6,4},{7,5},{8,10},{9,11},{10,... | collective-permute-start | bytes 680840 | tf_op jit(solution)/shard_map/ppermute | solution.py:832
  59.7 6.9 %collective-permute-start.19 = (bf16[3,192,197]{2,1,0:T(8,128)(2,1)S(1)}, bf16[3,192,197]{2,1,0:T(8,128)(2,1)S(1)}, u32[]{:S(2)}, u32[]{:S(2)}) collective-permute-start(bf16[3,192,197]{2,1,0:T(8,128)(2,1)S(1)} %get-tuple-element.241), channel_id=1, source_target_pairs={{0,1},{1,0},{2,3},{3,2},{4,5},{5,4},{6,7},{7,6},{8,9},{9,8},{10,11... | collective-permute-start | bytes 680840 | tf_op jit(solution)/shard_map/ppermute | solution.py:832
  63.8 5.6 %collective-permute-start.8 = (bf16[48,768]{1,0:T(8,128)(2,1)}, bf16[48,768]{1,0:T(8,128)(2,1)S(1)}, u32[]{:S(2)}, u32[]{:S(2)}) collective-permute-start(bf16[48,768]{1,0:T(8,128)(2,1)} %gate.14), channel_id=1, source_target_pairs={{0,16},{4,20},{8,24},{12,28},{16,0},{20,4},{24,8},{28,12},{1,17},{... | collective-permute-start | bytes 221192 | tf_op jit(solution)/shard_map/ppermute | solution.py:832
  66.6 9.6 %collective-permute-start.15 = (bf16[384,768]{1,0:T(8,128)(2,1)S(1)}, bf16[384,768]{1,0:T(8,128)(2,1)S(1)}, u32[]{:S(2)}, u32[]{:S(2)}) collective-permute-start(bf16[384,768]{1,0:T(8,128)(2,1)S(1)} %copy-done.14), channel_id=1, source_target_pairs={{0,1},{1,0},{2,3},{3,2},{4,5},{5,4},{6,7},{7,6},{8,9},{9,8},{10,11... | collective-permute-start | bytes 1769480 | tf_op jit(solution)/shard_map/ppermute | solution.py:832
  69.5 10.9 %collective-permute-start.16 = (bf16[384,768]{1,0:T(8,128)(2,1)S(1)}, bf16[384,768]{1,0:T(8,128)(2,1)S(1)}, u32[]{:S(2)}, u32[]{:S(2)}) collective-permute-start(bf16[384,768]{1,0:T(8,128)(2,1)S(1)} %copy-done.37), channel_id=1, source_target_pairs={{0,1},{1,0},{2,3},{3,2},{4,5},{5,4},{6,7},{7,6},{8,9},{9,8},{10,11... | collective-permute-start | bytes 1769480 | tf_op jit(solution)/shard_map/ppermute | solution.py:832
  74.7 4.3 %collective-permute-start.12 = (f32[12,768]{1,0:T(8,128)}, f32[12,768]{1,0:T(8,128)S(1)}, u32[]{:S(2)}, u32[]{:S(2)}) collective-permute-start(f32[12,768]{1,0:T(8,128)} %get-tuple-element.127.refs_4_), channel_id=1, source_target_pairs={{0,2},{1,3},{2,0},{3,1},{4,6},{5,7},{6,4},{7,5},{8,10},{9,11},{10,... | collective-permute-start | bytes 110600 | tf_op jit(solution)/shard_map/ppermute | solution.py:832
  76.1 4.2 %collective-permute-start.13 = (f32[12,768]{1,0:T(8,128)}, f32[12,768]{1,0:T(8,128)S(1)}, u32[]{:S(2)}, u32[]{:S(2)}) collective-permute-start(f32[12,768]{1,0:T(8,128)} %get-tuple-element.127.refs_4_), channel_id=1, source_target_pairs={{0,3},{1,2},{2,1},{3,0},{4,7},{5,6},{6,5},{7,4},{8,11},{9,10},{10,... | collective-permute-start | bytes 110600 | tf_op jit(solution)/shard_map/ppermute | solution.py:832
  76.3 29.3 %collective-permute-start.22 = (bf16[768,768]{1,0:T(8,128)(2,1)S(1)}, bf16[768,768]{1,0:T(8,128)(2,1)S(1)}, u32[]{:S(2)}, u32[]{:S(2)}) collective-permute-start(bf16[768,768]{1,0:T(8,128)(2,1)S(1)} %pad_maximum_fusion.1), channel_id=1, source_target_pairs={{0,2},{1,3},{2,0},{3,1},{4,6},{5,7},{6,4},{7,5},{8,10},{9,11},{10,... | collective-permute-start | bytes 3538952 | tf_op jit(solution)/shard_map/ppermute | solution.py:832
  106.6 28.2 %collective-permute-start.23 = (bf16[768,768]{1,0:T(8,128)(2,1)}, bf16[768,768]{1,0:T(8,128)(2,1)S(1)}, u32[]{:S(2)}, u32[]{:S(2)}) collective-permute-start(bf16[768,768]{1,0:T(8,128)(2,1)} %gate.15.refs_10_.refs_5_), channel_id=1, source_target_pairs={{0,4},{4,0},{8,12},{12,8},{16,20},{20,16},{24,28},{28,24},{1,5},{5... | collective-permute-start | bytes 3538952 | tf_op jit(solution)/shard_map/ppermute | solution.py:832
  135.8 4.7 %collective-permute-start.26 = (bf16[1536,768]{1,0:T(8,128)(2,1)}, bf16[1536,768]{1,0:T(8,128)(2,1)S(1)}, u32[]{:S(2)}, u32[]{:S(2)}) collective-permute-start(bf16[1536,768]{1,0:T(8,128)(2,1)} %get-tuple-element.136), channel_id=1, source_target_pairs={{0,1},{1,0},{2,3},{3,2},{4,5},{5,4},{6,7},{7,6},{8,9},{9,8},{10,11... | collective-permute-start | bytes 7077896 | tf_op jit(solution)/shard_map/ppermute | solution.py:832
  137.1 10.6 %collective-permute-start.24 = (bf16[768,768]{1,0:T(8,128)(2,1)S(1)}, bf16[768,768]{1,0:T(8,128)(2,1)S(1)}, u32[]{:S(2)}, u32[]{:S(2)}) collective-permute-start(bf16[768,768]{1,0:T(8,128)(2,1)S(1)} %copy-done.21), channel_id=1, source_target_pairs={{0,1},{1,0},{2,3},{3,2},{4,5},{5,4},{6,7},{7,6},{8,9},{9,8},{10,11... | collective-permute-start | bytes 3538952 | tf_op jit(solution)/shard_map/ppermute | solution.py:832
  137.1 10.6 %collective-permute-start.25 = (bf16[768,768]{1,0:T(8,128)(2,1)}, bf16[768,768]{1,0:T(8,128)(2,1)S(1)}, u32[]{:S(2)}, u32[]{:S(2)}) collective-permute-start(bf16[768,768]{1,0:T(8,128)(2,1)} %get-tuple-element.134.refs_6_), channel_id=1, source_target_pairs={{0,1},{1,0},{2,3},{3,2},{4,5},{5,4},{6,7},{7,6},{8,9},{9,8},{10,11... | collective-permute-start | bytes 3538952 | tf_op jit(solution)/shard_map/ppermute | solution.py:832
  145.3 23.8 %collective-permute-start.27 = (bf16[384,768]{1,0:T(8,128)(2,1)}, bf16[384,768]{1,0:T(8,128)(2,1)S(1)}, u32[]{:S(2)}, u32[]{:S(2)}) collective-permute-start(bf16[384,768]{1,0:T(8,128)(2,1)} %get-tuple-element.137.refs_9_), channel_id=1, source_target_pairs={{0,4},{4,0},{8,12},{12,8},{16,20},{20,16},{24,28},{28,24},{1,5},{5... | collective-permute-start | bytes 1769480 | tf_op jit(solution)/shard_map/ppermute | solution.py:832
  146.1 23.1 %collective-permute-start.28 = (bf16[384,768]{1,0:T(8,128)(2,1)}, bf16[384,768]{1,0:T(8,128)(2,1)S(1)}, u32[]{:S(2)}, u32[]{:S(2)}) collective-permute-start(bf16[384,768]{1,0:T(8,128)(2,1)} %get-tuple-element.138.refs_10_), channel_id=1, source_target_pairs={{0,8},{4,12},{8,0},{12,4},{16,24},{20,28},{24,16},{28,20},{1,9},{5... | collective-permute-start | bytes 1769480 | tf_op jit(solution)/shard_map/ppermute | solution.py:832
  173.2 4.8 %collective-permute-start.29 = (bf16[1536,768]{1,0:T(8,128)(2,1)}, bf16[1536,768]{1,0:T(8,128)(2,1)S(1)}, u32[]{:S(2)}, u32[]{:S(2)}) collective-permute-start(bf16[1536,768]{1,0:T(8,128)(2,1)} %get-tuple-element.155), channel_id=1, source_target_pairs={{0,1},{1,0},{2,3},{3,2},{4,5},{5,4},{6,7},{7,6},{8,9},{9,8},{10,11... | collective-permute-start | bytes 7077896 | tf_op jit(solution)/shard_map/ppermute | solution.py:832
  174.1 35.3 %collective-permute-start.30 = (bf16[192,768]{1,0:T(8,128)(2,1)S(1)}, bf16[192,768]{1,0:T(8,128)(2,1)S(1)}, u32[]{:S(2)}, u32[]{:S(2)}) collective-permute-start(bf16[192,768]{1,0:T(8,128)(2,1)S(1)} %copy-done.51), channel_id=1, source_target_pairs={{0,8},{4,12},{8,0},{12,4},{16,24},{20,28},{24,16},{28,20},{1,9},{5... | collective-permute-start | bytes 884744 | tf_op jit(solution)/shard_map/ppermute | solution.py:832
  174.6 34.9 %collective-permute-start.31 = (bf16[192,768]{1,0:T(8,128)(2,1)S(1)}, bf16[192,768]{1,0:T(8,128)(2,1)S(1)}, u32[]{:S(2)}, u32[]{:S(2)}) collective-permute-start(bf16[192,768]{1,0:T(8,128)(2,1)S(1)} %copy-done.50), channel_id=1, source_target_pairs={{0,16},{4,20},{8,24},{12,28},{16,0},{20,4},{24,8},{28,12},{1,17},{... | collective-permute-start | bytes 884744 | tf_op jit(solution)/shard_map/ppermute | solution.py:832
  182.7 30.4 %collective-permute-start.32 = (bf16[384,768]{1,0:T(8,128)(2,1)}, bf16[384,768]{1,0:T(8,128)(2,1)S(1)}, u32[]{:S(2)}, u32[]{:S(2)}) collective-permute-start(bf16[384,768]{1,0:T(8,128)(2,1)} %get-tuple-element.156.refs_14_), channel_id=1, source_target_pairs={{0,4},{4,0},{8,12},{12,8},{16,20},{20,16},{24,28},{28,24},{1,5},{5... | collective-permute-start | bytes 1769480 | tf_op jit(solution)/shard_map/ppermute | solution.py:832
  183.9 29.2 %collective-permute-start.33 = (bf16[384,768]{1,0:T(8,128)(2,1)}, bf16[384,768]{1,0:T(8,128)(2,1)S(1)}, u32[]{:S(2)}, u32[]{:S(2)}) collective-permute-start(bf16[384,768]{1,0:T(8,128)(2,1)} %get-tuple-element.157.refs_15_), channel_id=1, source_target_pairs={{0,8},{4,12},{8,0},{12,4},{16,24},{20,28},{24,16},{28,20},{1,9},{5... | collective-permute-start | bytes 1769480 | tf_op jit(solution)/shard_map/ppermute | solution.py:832
  217.1 14.2 %collective-permute-start.34 = (bf16[192,768]{1,0:T(8,128)(2,1)}, bf16[192,768]{1,0:T(8,128)(2,1)S(1)}, u32[]{:S(2)}, u32[]{:S(2)}) collective-permute-start(bf16[192,768]{1,0:T(8,128)(2,1)} %get-tuple-element.168.refs_2_), channel_id=1, source_target_pairs={{0,8},{4,12},{8,0},{12,4},{16,24},{20,28},{24,16},{28,20},{1,9},{5... | collective-permute-start | bytes 884744 | tf_op jit(solution)/shard_map/ppermute | solution.py:832
  217.8 16.7 %collective-permute-start.35 = (bf16[192,768]{1,0:T(8,128)(2,1)}, bf16[192,768]{1,0:T(8,128)(2,1)S(1)}, u32[]{:S(2)}, u32[]{:S(2)}) collective-permute-start(bf16[192,768]{1,0:T(8,128)(2,1)} %get-tuple-element.169.refs_3_), channel_id=1, source_target_pairs={{0,16},{4,20},{8,24},{12,28},{16,0},{20,4},{24,8},{28,12},{1,17},{... | collective-permute-start | bytes 884744 | tf_op jit(solution)/shard_map/ppermute | solution.py:832
  238.2 29.1 %collective-permute-start.38 = (bf16[768,768]{1,0:T(8,128)(2,1)}, bf16[768,768]{1,0:T(8,128)(2,1)S(1)}, u32[]{:S(2)}, u32[]{:S(2)}) collective-permute-start(bf16[768,768]{1,0:T(8,128)(2,1)} %get-tuple-element.178), channel_id=1, source_target_pairs={{0,1},{1,0},{2,3},{3,2},{4,5},{5,4},{6,7},{7,6},{8,9},{9,8},{10,11... | collective-permute-start | bytes 3538952 | tf_op jit(solution)/shard_map/ppermute | solution.py:832
  246.0 31.7 %collective-permute-start.37 = (bf16[768,768]{1,0:T(8,128)(2,1)}, bf16[768,768]{1,0:T(8,128)(2,1)S(1)}, u32[]{:S(2)}, u32[]{:S(2)}) collective-permute-start(bf16[768,768]{1,0:T(8,128)(2,1)} %added.19.refs_8_), channel_id=1, source_target_pairs={{0,2},{1,3},{2,0},{3,1},{4,6},{5,7},{6,4},{7,5},{8,10},{9,11},{10,... | collective-permute-start | bytes 3538952 | tf_op jit(solution)/shard_map/ppermute | solution.py:832
  246.7 14.2 %collective-permute-start.39 = (bf16[96,768]{1,0:T(8,128)(2,1)S(1)}, bf16[96,768]{1,0:T(8,128)(2,1)S(1)}, u32[]{:S(2)}, u32[]{:S(2)}) collective-permute-start(bf16[96,768]{1,0:T(8,128)(2,1)S(1)} %copy-done.53), channel_id=1, source_target_pairs={{0,16},{4,20},{8,24},{12,28},{16,0},{20,4},{24,8},{28,12},{1,17},{... | collective-permute-start | bytes 442376 | tf_op jit(solution)/shard_map/ppermute | solution.py:832
  246.7 15.7 %collective-permute-start.40 = (bf16[96,768]{1,0:T(8,128)(2,1)S(1)}, bf16[96,768]{1,0:T(8,128)(2,1)S(1)}, u32[]{:S(2)}, u32[]{:S(2)}) collective-permute-start(bf16[96,768]{1,0:T(8,128)(2,1)S(1)} %copy-done.95), channel_id=1, source_target_pairs={{0,4},{4,0},{8,12},{12,8},{16,20},{20,16},{24,28},{28,24},{1,5},{5... | collective-permute-start | bytes 442376 | tf_op jit(solution)/shard_map/ppermute | solution.py:832
  248.3 19.0 %collective-permute-start.41 = (bf16[96,768]{1,0:T(8,128)(2,1)S(1)}, bf16[96,768]{1,0:T(8,128)(2,1)S(1)}, u32[]{:S(2)}, u32[]{:S(2)}) collective-permute-start(bf16[96,768]{1,0:T(8,128)(2,1)S(1)} %copy-done.40), channel_id=1, source_target_pairs={{0,16},{4,20},{8,24},{12,28},{16,0},{20,4},{24,8},{28,12},{1,17},{... | collective-permute-start | bytes 442376 | tf_op jit(solution)/shard_map/ppermute | solution.py:832
  260.9 6.3 %collective-permute-start.42 = (bf16[96,768]{1,0:T(8,128)(2,1)S(1)}, bf16[96,768]{1,0:T(8,128)(2,1)S(1)}, u32[]{:S(2)}, u32[]{:S(2)}) collective-permute-start(bf16[96,768]{1,0:T(8,128)(2,1)S(1)} %copy-done.59), channel_id=1, source_target_pairs={{0,4},{4,0},{8,12},{12,8},{16,20},{20,16},{24,28},{28,24},{1,5},{5... | collective-permute-start | bytes 442376 | tf_op jit(solution)/shard_map/ppermute | solution.py:832
  266.1 17.7 %collective-permute-start.45 = (bf16[192,768]{1,0:T(8,128)(2,1)}, bf16[192,768]{1,0:T(8,128)(2,1)S(1)}, u32[]{:S(2)}, u32[]{:S(2)}) collective-permute-start(bf16[192,768]{1,0:T(8,128)(2,1)} %added.20.refs_2_), channel_id=1, source_target_pairs={{0,2},{1,3},{2,0},{3,1},{4,6},{5,7},{6,4},{7,5},{8,10},{9,11},{10,... | collective-permute-start | bytes 884744 | tf_op jit(solution)/shard_map/ppermute | solution.py:832
  281.7 7.9 %collective-permute-start.43 = (bf16[192,768]{1,0:T(8,128)(2,1)}, bf16[192,768]{1,0:T(8,128)(2,1)S(1)}, u32[]{:S(2)}, u32[]{:S(2)}) collective-permute-start(bf16[192,768]{1,0:T(8,128)(2,1)} %get-tuple-element.182.refs_9_), channel_id=1, source_target_pairs={{0,4},{4,0},{8,12},{12,8},{16,20},{20,16},{24,28},{28,24},{1,5},{5... | collective-permute-start | bytes 884744 | tf_op jit(solution)/shard_map/ppermute | solution.py:832
  282.7 8.3 %collective-permute-start.44 = (bf16[192,768]{1,0:T(8,128)(2,1)}, bf16[192,768]{1,0:T(8,128)(2,1)S(1)}, u32[]{:S(2)}, u32[]{:S(2)}) collective-permute-start(bf16[192,768]{1,0:T(8,128)(2,1)} %get-tuple-element.183), channel_id=1, source_target_pairs={{0,8},{4,12},{8,0},{12,4},{16,24},{20,28},{24,16},{28,20},{1,9},{5... | collective-permute-start | bytes 884744 | tf_op jit(solution)/shard_map/ppermute | solution.py:832
  299.7 5.2 %collective-permute-start.51 = (f32[96,768]{1,0:T(8,128)}, f32[96,768]{1,0:T(8,128)S(1)}, u32[]{:S(2)}, u32[]{:S(2)}) collective-permute-start(f32[96,768]{1,0:T(8,128)} %get-tuple-element.196.refs_1_), channel_id=1, source_target_pairs={{0,1},{1,0},{2,3},{3,2},{4,5},{5,4},{6,7},{7,6},{8,9},{9,8},{10,11... | collective-permute-start | bytes 884744 | tf_op jit(solution)/shard_map/ppermute | solution.py:832
  299.7 20.0 %collective-permute-start.54 = (bf16[96,768]{1,0:T(8,128)(2,1)S(1)}, bf16[96,768]{1,0:T(8,128)(2,1)S(1)}, u32[]{:S(2)}, u32[]{:S(2)}) collective-permute-start(bf16[96,768]{1,0:T(8,128)(2,1)S(1)} %copy-done.35), channel_id=1, source_target_pairs={{0,16},{4,20},{8,24},{12,28},{16,0},{20,4},{24,8},{28,12},{1,17},{... | collective-permute-start | bytes 442376 | tf_op jit(solution)/shard_map/ppermute | solution.py:832
  302.1 17.7 %collective-permute-start.55 = (bf16[96,768]{1,0:T(8,128)(2,1)S(1)}, bf16[96,768]{1,0:T(8,128)(2,1)S(1)}, u32[]{:S(2)}, u32[]{:S(2)}) collective-permute-start(bf16[96,768]{1,0:T(8,128)(2,1)S(1)} %copy-done.54), channel_id=1, source_target_pairs={{0,4},{4,0},{8,12},{12,8},{16,20},{20,16},{24,28},{28,24},{1,5},{5... | collective-permute-start | bytes 442376 | tf_op jit(solution)/shard_map/ppermute | solution.py:832
  302.5 8.7 %collective-permute-start.49 = (bf16[96,768]{1,0:T(8,128)(2,1)S(1)}, bf16[96,768]{1,0:T(8,128)(2,1)S(1)}, u32[]{:S(2)}, u32[]{:S(2)}) collective-permute-start(bf16[96,768]{1,0:T(8,128)(2,1)S(1)} %copy-done.32), channel_id=1, source_target_pairs={{0,8},{4,12},{8,0},{12,4},{16,24},{20,28},{24,16},{28,20},{1,9},{5... | collective-permute-start | bytes 442376 | tf_op jit(solution)/shard_map/ppermute | solution.py:832
  304.2 12.2 %collective-permute-start.50 = (bf16[96,768]{1,0:T(8,128)(2,1)S(1)}, bf16[96,768]{1,0:T(8,128)(2,1)S(1)}, u32[]{:S(2)}, u32[]{:S(2)}) collective-permute-start(bf16[96,768]{1,0:T(8,128)(2,1)S(1)} %copy-done.94), channel_id=1, source_target_pairs={{0,16},{4,20},{8,24},{12,28},{16,0},{20,4},{24,8},{28,12},{1,17},{... | collective-permute-start | bytes 442376 | tf_op jit(solution)/shard_map/ppermute | solution.py:832
  323.2 25.3 %collective-permute-start.58 = (bf16[192,768]{1,0:T(8,128)(2,1)}, bf16[192,768]{1,0:T(8,128)(2,1)S(1)}, u32[]{:S(2)}, u32[]{:S(2)}) collective-permute-start(bf16[192,768]{1,0:T(8,128)(2,1)} %get-tuple-element.200.refs_9_.refs_0_), channel_id=1, source_target_pairs={{0,8},{4,12},{8,0},{12,4},{16,24},{20,28},{24,16},{28,20},{1,9},{5... | collective-permute-start | bytes 884744 | tf_op jit(solution)/shard_map/ppermute | solution.py:832
  323.6 24.9 %collective-permute-start.59 = (bf16[192,768]{1,0:T(8,128)(2,1)}, bf16[192,768]{1,0:T(8,128)(2,1)S(1)}, u32[]{:S(2)}, u32[]{:S(2)}) collective-permute-start(bf16[192,768]{1,0:T(8,128)(2,1)} %get-tuple-element.203.refs_2_), channel_id=1, source_target_pairs={{0,16},{4,20},{8,24},{12,28},{16,0},{20,4},{24,8},{28,12},{1,17},{... | collective-permute-start | bytes 884744 | tf_op jit(solution)/shard_map/ppermute | solution.py:832
  326.9 16.7 %collective-permute-start.52 = (bf16[48,768]{1,0:T(8,128)(2,1)}, bf16[48,768]{1,0:T(8,128)(2,1)S(1)}, u32[]{:S(2)}, u32[]{:S(2)}) collective-permute-start(bf16[48,768]{1,0:T(8,128)(2,1)} %get-tuple-element.197.refs_4_), channel_id=1, source_target_pairs={{0,16},{4,20},{8,24},{12,28},{16,0},{20,4},{24,8},{28,12},{1,17},{... | collective-permute-start | bytes 221192 | tf_op jit(solution)/shard_map/ppermute | solution.py:832
  327.0 16.7 %collective-permute-start.53 = (bf16[48,768]{1,0:T(8,128)(2,1)}, bf16[48,768]{1,0:T(8,128)(2,1)S(1)}, u32[]{:S(2)}, u32[]{:S(2)}) collective-permute-start(bf16[48,768]{1,0:T(8,128)(2,1)} %get-tuple-element.198), channel_id=1, source_target_pairs={{0,4},{4,0},{8,12},{12,8},{16,20},{20,16},{24,28},{28,24},{1,5},{5... | collective-permute-start | bytes 221192 | tf_op jit(solution)/shard_map/ppermute | solution.py:832
  327.4 19.7 %collective-permute-start.60 = (bf16[96,768]{1,0:T(8,128)(2,1)S(1)}, bf16[96,768]{1,0:T(8,128)(2,1)S(1)}, u32[]{:S(2)}, u32[]{:S(2)}) collective-permute-start(bf16[96,768]{1,0:T(8,128)(2,1)S(1)} %get-tuple-element.237), channel_id=1, source_target_pairs={{0,2},{1,3},{2,0},{3,1},{4,6},{5,7},{6,4},{7,5},{8,10},{9,11},{10,... | collective-permute-start | bytes 442376 | tf_op jit(solution)/shard_map/ppermute | solution.py:832
  343.6 22.7 %collective-permute-start.46 = (bf16[3,2,192,197]{3,2,1,0:T(8,128)(2,1)}, bf16[3,2,192,197]{3,2,1,0:T(8,128)(2,1)S(1)}, u32[]{:S(2)}, u32[]{:S(2)}) collective-permute-start(bf16[3,2,192,197]{3,2,1,0:T(8,128)(2,1)} %get-tuple-element.187), channel_id=1, source_target_pairs={{0,1},{1,0},{2,3},{3,2},{4,5},{5,4},{6,7},{7,6},{8,9},{9,8},{10,11... | collective-permute-start | bytes 1361672 | tf_op jit(solution)/shard_map/ppermute | solution.py:832
  343.6 22.8 %collective-permute-start.47 = (bf16[3,2,192,197]{3,2,1,0:T(8,128)(2,1)}, bf16[3,2,192,197]{3,2,1,0:T(8,128)(2,1)S(1)}, u32[]{:S(2)}, u32[]{:S(2)}) collective-permute-start(bf16[3,2,192,197]{3,2,1,0:T(8,128)(2,1)} %get-tuple-element.188), channel_id=1, source_target_pairs={{0,2},{1,3},{2,0},{3,1},{4,6},{5,7},{6,4},{7,5},{8,10},{9,11},{10,... | collective-permute-start | bytes 1361672 | tf_op jit(solution)/shard_map/ppermute | solution.py:832
  347.2 24.6 %collective-permute-start.48 = (bf16[3,2,192,197]{3,2,1,0:T(8,128)(2,1)S(1)}, bf16[3,2,192,197]{3,2,1,0:T(8,128)(2,1)S(1)}, u32[]{:S(2)}, u32[]{:S(2)}) collective-permute-start(bf16[3,2,192,197]{3,2,1,0:T(8,128)(2,1)S(1)} %copy-done.33), channel_id=1, source_target_pairs={{0,3},{1,2},{2,1},{3,0},{4,7},{5,6},{6,5},{7,4},{8,11},{9,10},{10,... | collective-permute-start | bytes 1361672 | tf_op jit(solution)/shard_map/ppermute | solution.py:832
  348.5 8.3 %collective-permute-start.56 = (bf16[48,768]{1,0:T(8,128)(2,1)}, bf16[48,768]{1,0:T(8,128)(2,1)S(1)}, u32[]{:S(2)}, u32[]{:S(2)}) collective-permute-start(bf16[48,768]{1,0:T(8,128)(2,1)} %get-tuple-element.201.refs_1_.refs_0_), channel_id=1, source_target_pairs={{0,16},{4,20},{8,24},{12,28},{16,0},{20,4},{24,8},{28,12},{1,17},{... | collective-permute-start | bytes 221192 | tf_op jit(solution)/shard_map/ppermute | solution.py:832
  348.5 10.0 %collective-permute-start.57 = (bf16[48,768]{1,0:T(8,128)(2,1)}, bf16[48,768]{1,0:T(8,128)(2,1)S(1)}, u32[]{:S(2)}, u32[]{:S(2)}) collective-permute-start(bf16[48,768]{1,0:T(8,128)(2,1)} %get-tuple-element.202.refs_2_), channel_id=1, source_target_pairs={{0,4},{4,0},{8,12},{12,8},{16,20},{20,16},{24,28},{28,24},{1,5},{5... | collective-permute-start | bytes 221192 | tf_op jit(solution)/shard_map/ppermute | solution.py:832
  356.8 41.3 %collective-permute-start.65 = (bf16[384,768]{1,0:T(8,128)(2,1)}, bf16[384,768]{1,0:T(8,128)(2,1)S(1)}, u32[]{:S(2)}, u32[]{:S(2)}) collective-permute-start(bf16[384,768]{1,0:T(8,128)(2,1)} %get-tuple-element.208.refs_4_.refs_0_), channel_id=1, source_target_pairs={{0,4},{4,0},{8,12},{12,8},{16,20},{20,16},{24,28},{28,24},{1,5},{5... | collective-permute-start | bytes 1769480 | tf_op jit(solution)/shard_map/ppermute | solution.py:832
  359.1 39.0 %collective-permute-start.66 = (bf16[384,768]{1,0:T(8,128)(2,1)}, bf16[384,768]{1,0:T(8,128)(2,1)S(1)}, u32[]{:S(2)}, u32[]{:S(2)}) collective-permute-start(bf16[384,768]{1,0:T(8,128)(2,1)} %get-tuple-element.227.refs_2_), channel_id=1, source_target_pairs={{0,8},{4,12},{8,0},{12,4},{16,24},{20,28},{24,16},{28,20},{1,9},{5... | collective-permute-start | bytes 1769480 | tf_op jit(solution)/shard_map/ppermute | solution.py:832
  366.4 15.2 %collective-permute-start.61 = (bf16[96,768]{1,0:T(8,128)(2,1)}, bf16[96,768]{1,0:T(8,128)(2,1)S(1)}, u32[]{:S(2)}, u32[]{:S(2)}) collective-permute-start(bf16[96,768]{1,0:T(8,128)(2,1)} %get-tuple-element.209.refs_3_.refs_0_), channel_id=1, source_target_pairs={{0,8},{4,12},{8,0},{12,4},{16,24},{20,28},{24,16},{28,20},{1,9},{5... | collective-permute-start | bytes 442376 | tf_op jit(solution)/shard_map/ppermute | solution.py:832
  366.5 15.1 %collective-permute-start.62 = (bf16[96,768]{1,0:T(8,128)(2,1)}, bf16[96,768]{1,0:T(8,128)(2,1)S(1)}, u32[]{:S(2)}, u32[]{:S(2)}) collective-permute-start(bf16[96,768]{1,0:T(8,128)(2,1)} %get-tuple-element.222.refs_2_), channel_id=1, source_target_pairs={{0,16},{4,20},{8,24},{12,28},{16,0},{20,4},{24,8},{28,12},{1,17},{... | collective-permute-start | bytes 442376 | tf_op jit(solution)/shard_map/ppermute | solution.py:832
  384.9 8.1 %collective-permute-start.63 = (bf16[192,768]{1,0:T(8,128)(2,1)}, bf16[192,768]{1,0:T(8,128)(2,1)S(1)}, u32[]{:S(2)}, u32[]{:S(2)}) collective-permute-start(bf16[192,768]{1,0:T(8,128)(2,1)} %get-tuple-element.223.refs_0_.refs_4_), channel_id=1, source_target_pairs={{0,4},{4,0},{8,12},{12,8},{16,20},{20,16},{24,28},{28,24},{1,5},{5... | collective-permute-start | bytes 884744 | tf_op jit(solution)/shard_map/ppermute | solution.py:832
  385.8 8.1 %collective-permute-start.64 = (bf16[192,768]{1,0:T(8,128)(2,1)}, bf16[192,768]{1,0:T(8,128)(2,1)S(1)}, u32[]{:S(2)}, u32[]{:S(2)}) collective-permute-start(bf16[192,768]{1,0:T(8,128)(2,1)} %get-tuple-element.224.refs_2_), channel_id=1, source_target_pairs={{0,8},{4,12},{8,0},{12,4},{16,24},{20,28},{24,16},{28,20},{1,9},{5... | collective-permute-start | bytes 884744 | tf_op jit(solution)/shard_map/ppermute | solution.py:832
  (104 other events, 410.0 us)
Sparse Core Ops, SparseCore 0:
  221.2 60.4 all-gather.2
